TPU v7x, 512 devices: a whole 4x4x16 slice. The times are simulated.
512 devices in a mesh: rows: 128 (over y, z, core), grp: 4 (over x).
Axes of the slice: x: 4, y: 4, z: 16, core: 2. Of those that a mesh axis runs over, the one named last changes fastest.
Arguments:
- embeddings: float32 [114688, 4096], P(('rows', 'grp')), may hold values from -108 to 108
- test_matrix: bfloat16 [4096, 128], replicated, may hold values from -0.09375 to 0.09375
Outputs:
- basis: float32 [114688, 128], P(('rows', 'grp'))
- right_basis: float32 [4096, 128], P(('rows', 'grp'))
- factor: float32 [128, 128], replicated
All inputs are finite; a program needn't handle non-finite values.
Results may differ from a plain program's by a relative error of at most 0.0003.
Values sent between devices are 32-bit elements; how exact they have to be, the bound alone decides.
No kernel may reach another device: no remote copies, remote signals or barrier semaphores. Data moves between devices by JAX's collectives and lax.ppermute only.
A program may use at most 64 MiB of HBM per device.

v0:
```python
import jax
import jax.numpy as jnp
from jax import lax
from jax.sharding import PartitionSpec as P


def local_gram(values):
    return lax.dot_general(
        values,
        values,
        (((0,), (0,)), ((), ())),
        precision=lax.Precision.HIGHEST,
        preferred_element_type=jnp.float32,
    )


def total_gram(partial_value):
    return lax.psum(partial_value, ("rows", "grp"))


def lower_solve(lower, values):
    return lax.linalg.triangular_solve(lower, values, left_side=False, lower=True, transpose_a=True)


def per_device(embeddings, test_matrix):
    devices_all = lax.axis_size(("rows", "grp"))
    total_rows = embeddings.shape[0] * devices_all
    width = embeddings.shape[1]
    sketch = jnp.dot(
        embeddings,
        test_matrix.astype(jnp.float32),
        precision=lax.Precision.HIGHEST,
        preferred_element_type=jnp.float32,
    )
    lower_first = jnp.linalg.cholesky(total_gram(local_gram(sketch)) / total_rows)
    basis = lower_solve(lower_first, sketch)
    loadings = lax.psum_scatter(
        lax.dot_general(
            embeddings,
            basis,
            (((0,), (0,)), ((), ())),
            precision=lax.Precision.HIGHEST,
            preferred_element_type=jnp.float32,
        ),
        ("rows", "grp"),
        scatter_dimension=0,
        tiled=True,
    )
    factor = jnp.linalg.cholesky(total_gram(local_gram(loadings)) / width)
    right_basis = lower_solve(factor, loadings)
    return (basis, right_basis, factor)


def solution(mesh):
    return jax.shard_map(
        per_device,
        mesh=mesh,
        in_specs=(P(("rows", "grp"), None), P()),
        out_specs=(P(("rows", "grp"), None), P(("rows", "grp"), None), P()),
        check_vma=False,
    )
```

profile of v0, /device:TPU:1, one launch (start us, length us, event | category | flops | bytes accessed | tf_op | source)
XLA Modules:
  0.0 1434.8 jit_solution(884208726310594012)
XLA Ops:
  7.2 0.0 copy-start
  7.2 0.0 all-reduce.5.cloned.1.call-start
  7.2 1.2 copy-done
  8.4 3.8 fusion.12
  12.2 1.0 fusion.13
  13.2 0.0 all-reduce.5.cloned.1.call-update
  13.2 0.0 all-reduce.9.cloned.1.call-start
  13.3 445.8 %all-reduce.5.cloned.1.call-done = f32[128,128]{0,1:T(8,128)} async-done(((f32[128,128]{0,1:T(8,128)}), f32[128,128]{0,1:T(8,128)}) %all-reduce.5.cloned.1.call-update) | async-done | bytes 65552 | tf_op jit(solution)/shard_map/psum | solution.py:18
  459.0 0.8 broadcast_multiply_fusion.1
  459.9 0.1 copy.10
  460.0 0.9 fusion.6
  460.8 11.7 cholesky.44
  472.6 0.6 compare_reduce_fusion.1
  473.2 0.7 fusion
  473.9 9.8 custom-call.8
  483.7 0.3 fusion.4
  484.0 0.0 copy-start.1
  484.0 5.5 convolution_bitcast_fusion
  489.5 0.0 all-reduce.9.cloned.1.call-update
  489.5 0.0 copy-done.1
  489.5 0.2 all-reduce.7.cloned.1.call-start
  489.7 466.8 %all-reduce.9.cloned.1.call-done = f32[4096,128]{0,1:T(8,128)} async-done(((f32[4096,128]{0,1:T(8,128)}), f32[4096,128]{0,1:T(8,128)}) %all-reduce.9.cloned.1.call-update) | async-done | bytes 2097168
  956.6 1.9 fusion.8
  958.4 0.0 all-reduce.7.cloned.1.call-update
  958.5 442.8 %all-reduce.7.cloned.1.call-done = f32[128,128]{0,1:T(8,128)} async-done(((f32[128,128]{0,1:T(8,128)}), f32[128,128]{0,1:T(8,128)}) %all-reduce.7.cloned.1.call-update) | async-done | bytes 65552 | tf_op jit(solution)/shard_map/psum | solution.py:18
  1401.2 0.8 broadcast_multiply_fusion
  1402.1 0.1 copy.12
  1402.2 0.9 fusion.3
  1403.0 11.7 cholesky.55
  1414.8 0.6 compare_reduce_fusion
  1415.4 1.3 select_bitcast_fusion
  1416.7 9.8 custom-call.9
  1426.5 1.8 fusion.1
  (2 shorter events, 0.1 us)
Async XLA Ops:
  7.2 1.2 copy-start
  7.2 451.9 %all-reduce.5.cloned.1.call-start = ((), (), s32[]{:S(2)}) async-start(), calls=%async_computation | async-start | bytes 131072 | tf_op jit(solution)/shard_map/psum | solution.py:18
  13.2 943.3 %all-reduce.9.cloned.1.call-start = ((), (), s32[]{:S(2)}) async-start(), calls=%async_computation.2 | async-start | bytes 4194304
  484.0 5.5 copy-start.1
  489.5 911.7 %all-reduce.7.cloned.1.call-start = ((), (), s32[]{:S(2)}) async-start(), calls=%async_computation.1 | async-start | bytes 131072 | tf_op jit(solution)/shard_map/psum | solution.py:18
Sparse Core Ops, SparseCore 0:
  14.0 444.9 all-reduce.4
  489.6 466.8 all-reduce.8
  963.5 437.7 all-reduce.6
where the time goes:
time: 1440 us; the launch traced here: 1430 us
  waiting for transfers between devices  1360 us (94%)
  other arithmetic  49.7 us (3%)
    psum x2, waiting for transfers between devices, total_gram(): return lax.psum(partial_value, ('rows', 'grp'))  889 us
    unnamed x4, waiting for transfers between devices  467 us
  transfers between devices with their start and end apart: 3, of which 3 were waited for; matrix products, arithmetic and copies ran while one was open for 0% of the time, Pallas kernels for 0%

commit v1 on v0

v1 whole, which is shorter than its diff:
```python
import jax
import jax.numpy as jnp
from jax import lax
from jax.sharding import Mesh, PartitionSpec as P

HIGHEST = lax.Precision.HIGHEST
AXES = ("y", "z", "core", "x")


def exchange(values, axes):
    return lax.all_to_all(values, axes, 0, 0, tiled=False)


def reduce_scatter(values, axes):
    parts = lax.axis_size(axes)
    blocks = values.reshape((parts, values.shape[0] // parts) + values.shape[1:])
    return jnp.sum(exchange(blocks, axes), axis=0)


def gather(values, axes):
    parts = lax.axis_size(axes)
    copies = jnp.broadcast_to(values[None], (parts,) + values.shape)
    blocks = exchange(copies, axes)
    return blocks.reshape((parts * values.shape[0],) + values.shape[1:])


def lower_solve(lower, values):
    return lax.linalg.triangular_solve(lower, values, left_side=False, lower=True, transpose_a=True)


def dot(left, right, left_dim, right_dim):
    return lax.dot_general(
        left,
        right,
        (((left_dim,), (right_dim,)), ((), ())),
        precision=HIGHEST,
        preferred_element_type=jnp.float32,
    )


def per_device(embeddings, test_matrix):
    devices_all = lax.axis_size(AXES)
    total_rows = embeddings.shape[0] * devices_all
    width = embeddings.shape[1]
    own_rows = width // devices_all
    test = test_matrix.astype(jnp.float32)
    sketch = dot(embeddings, test, 1, 0)
    image = dot(embeddings, sketch, 0, 0)
    image = reduce_scatter(image, "core")
    image = reduce_scatter(image, ("x", "y"))
    image = reduce_scatter(image, "z")
    image = gather(image, "z")
    image = gather(image, ("x", "y"))
    image = gather(image, "core")
    lower_first = jnp.linalg.cholesky(dot(test, image, 0, 0) / total_rows, symmetrize_input=False)
    basis = lower_solve(lower_first, sketch)
    loadings = lower_solve(lower_first, image)
    factor = jnp.linalg.cholesky(dot(loadings, loadings, 0, 0) / width, symmetrize_input=False)
    own = lax.dynamic_slice_in_dim(loadings, lax.axis_index(AXES) * own_rows, own_rows, 0)
    right_basis = lower_solve(factor, own)
    return (basis, right_basis, factor)


def solution(mesh):
    fine = Mesh(mesh.devices.reshape(4, 16, 2, 4), AXES)
    return jax.shard_map(
        per_device,
        mesh=fine,
        in_specs=(P(AXES, None), P()),
        out_specs=(P(AXES, None), P(AXES, None), P()),
        check_vma=False,
    )
```

time: 1440 us -> 167 us (0.12)
  waiting for transfers between devices: 1360 us -> 12 us
  blocking collectives: 0 us -> 81 us
    psum x2 -> x0, waiting for transfers between devices: 889 us -> none  [total_gram(): return lax.psum(partial_value, ('rows', 'grp'))]
    unnamed x4 -> x0, waiting for transfers between devices: 467 us -> none
    all_to_all x0 -> x5, blocking collectives: none -> 81 us  [exchange(): return lax.all_to_all(values, axes, 0, 0, tiled=False)]
  transfers between devices with their start and end apart: 3 -> 1, of which waited for: 3 -> 1; matrix products, arithmetic and copies ran while one was open for 0% -> 0% of each run, Pallas kernels for 0% -> 0%
where the time goes in v1:
time: 167 us
  blocking collectives  81 us (49%)
  other arithmetic  47.6 us (29%)
  matrix products  16.2 us (10%)
  waiting for transfers between devices  12 us (7%)
  local copies, waits for them, and re-layouts  5.35 us (3%)
  starting transfers between devices  3.73 us (2%)
    all_to_all x5, blocking collectives, exchange(): return lax.all_to_all(values, axes, 0, 0, tiled=False)  81 us
    another operation x4, other arithmetic, lower_solve(): lax.linalg.triangular_solve(lower, values, left_side=False, lower=True, t...  21.6 us
    another operation x3, other arithmetic, per_device(): jnp.linalg.cholesky(dot(loadings, loadings, 0, 0) / width, symmetrize_inp...  12.4 us
    another operation x3, other arithmetic, per_device(): jnp.linalg.cholesky(dot(test, image, 0, 0) / total_rows, symmetrize_input...  12.4 us
    all_to_all x1, waiting for transfers between devices, exchange(): return lax.all_to_all(values, axes, 0, 0, tiled=False)  12 us
    dot_general x4, matrix products, dot(): lax.dot_general(left, right, (((left_dim,), (right_dim,)), ((), ())), pre...  11.2 us
    another operation x3, matrix products, lower_solve(): lax.linalg.triangular_solve(lower, values, left_side=False, lower=True, t...  5.04 us
    all_to_all x1, starting transfers between devices, exchange(): return lax.all_to_all(values, axes, 0, 0, tiled=False)  3.73 us
  transfers between devices with their start and end apart: 1, of which 1 were waited for; matrix products, arithmetic and copies ran while one was open for 0% of the time, Pallas kernels for 0%

profile of v1, /device:TPU:1, one launch (start us, length us, event | category | flops | bytes accessed | tf_op | source)
XLA Modules:
  0.0 166.7 jit_solution(17324968765491445014)
XLA Ops:
  0.6 0.0 copy-start
  0.6 0.0 copy-start.2
  0.7 1.2 copy-done
  1.9 3.9 %fusion.10 = f32[224,128]{1,0:T(8,128)S(1)} fusion(f32[224,4096]{1,0:T(8,128)} %param.3, bf16[4096,128]{1,0:T(8,128)(2,1)S(1)} %copy-done), kind=kOutput, calls=%fused_computation.23 | convolution fusion | flops 1409286144 | bytes 4833280 | tf_op jit(solution)/shard_map/dot_general | solution.py:32
  5.8 0.0 copy-done.2
  5.8 2.2 %fusion.11 = f32[128,4096]{1,0:T(8,128)S(1)} fusion(f32[224,128]{1,0:T(8,128)S(1)} %fusion.10, f32[224,4096]{1,0:T(8,128)S(1)} %copy-done.2), kind=kOutput, calls=%fused_computation.24 | convolution fusion | flops 1409286144 | bytes 5881856 | tf_op jit(solution)/shard_map/dot_general | solution.py:32
  8.0 0.1 copy.27
  8.2 11.9 %all_to_all.30 = f32[2,2048,128]{1,2,0:T(8,128)S(1)} all-to-all(f32[2,2048,128]{1,2,0:T(8,128)S(1)} %bitcast.41), channel_id=1, replica_groups=mesh['y'=4,'z'=16,'core'=2,'x'=4] {'core'}, dimensions={0} | all-to-all | bytes 4194304 | tf_op jit(solution)/shard_map/all_to_all | solution.py:11
  20.1 1.2 reduce_sum.27
  21.3 1.3 copy_bitcast_fusion.1
  22.6 18.5 %all_to_all.31 = f32[16,128,128]{1,2,0:T(8,128)S(1)} all-to-all(f32[16,128,128]{1,2,0:T(8,128)S(1)} %copy_bitcast_fusion.1), channel_id=1, replica_groups=mesh['y'=4,'z'=16,'core'=2,'x'=4] {'x','y'}, dimensions={0} | all-to-all | bytes 2097152 | tf_op jit(solution)/shard_map/all_to_all | solution.py:11
  41.1 0.1 reduce_sum.28
  41.2 0.1 copy.18
  41.3 25.0 %all_to_all.32 = f32[16,8,128]{2,1,0:T(8,128)S(1)} all-to-all(f32[16,8,128]{2,1,0:T(8,128)S(1)} %bitcast.44), channel_id=1, replica_groups=mesh['y'=4,'z'=16,'core'=2,'x'=4] {'z'}, dimensions={0} | all-to-all | bytes 131072 | tf_op jit(solution)/shard_map/all_to_all | solution.py:11
  66.3 14.3 %all_to_all.33 = f32[16,8,128]{2,1,0:T(8,128)S(1)} all-to-all(f32[16,8,128]{2,1,0:T(8,128)S(1)} %broadcast_in_dim.10), channel_id=1, replica_groups=mesh['y'=4,'z'=16,'core'=2,'x'=4] {'z'}, dimensions={0} | all-to-all | bytes 131072 | tf_op jit(solution)/shard_map/all_to_all | solution.py:11
  80.7 1.1 broadcast_in_dim.23
  81.7 3.7 %all-to-all-start.4 = ((f32[16,128,128]{2,1,0:T(8,128)}), f32[16,128,128]{2,1,0:T(8,128)S(1)}, u32[]{:S(2)}, u32[]{:S(2)}) async-start(f32[16,128,128]{2,1,0:T(8,128)} %broadcast_in_dim.23), calls=%async_computation.4 | async-start | bytes 2097152 | tf_op jit(solution)/shard_map/all_to_all | solution.py:11
  85.5 12.0 %all-to-all-done.4 = f32[16,128,128]{2,1,0:T(8,128)S(1)} async-done(((f32[16,128,128]{2,1,0:T(8,128)}), f32[16,128,128]{2,1,0:T(8,128)S(1)}, u32[]{:S(2)}, u32[]{:S(2)}) %all-to-all-start.4) | async-done | bytes 1048608 | tf_op jit(solution)/shard_map/all_to_all | solution.py:11
  97.5 0.1 broadcast_in_dim.25
  97.6 11.2 %all_to_all.34 = f32[2,2048,128]{2,1,0:T(8,128)S(1)} all-to-all(f32[2,2048,128]{2,1,0:T(8,128)S(1)} %broadcast_in_dim.25), channel_id=1, replica_groups=mesh['y'=4,'z'=16,'core'=2,'x'=4] {'core'}, dimensions={0} | all-to-all | bytes 4194304 | tf_op jit(solution)/shard_map/all_to_all | solution.py:11
  108.8 0.0 copy-start.1
  108.8 1.3 copy-done.1
  110.2 1.4 fusion
  111.6 11.7 %cholesky.45 = f32[128,128]{1,0:T(8,128)S(1)} custom-call(f32[128,128]{1,0:T(8,128)S(1)} %fusion), custom_call_target="Cholesky" | custom-call | tf_op jit(solution)/shard_map/jit(cholesky)/cholesky | solution.py:55
  123.3 0.6 compare_reduce_fusion.1
  124.0 0.7 fusion.1
  124.6 9.8 %custom-call.10 = f32[1,128,128]{1,2,0:T(8,128)S(1)} custom-call(f32[1,128,128]{2,1,0:T(8,128)S(1)} %fusion.1), custom_call_target="InvertDiagBlocksLowerTriangular" | custom-call | tf_op jit(solution)/shard_map/triangular_solve | solution.py:28
  134.5 0.9 fusion.6
  135.4 3.4 %fusion.4 = f32[4096,128]{1,0:T(8,128)S(1)} fusion(f32[4096,128]{1,0:T(8,128)} %bitcast.39, f32[1,128,128]{1,2,0:T(8,128)S(1)} %custom-call.10), kind=kOutput, calls=%fused_computation.9 | convolution fusion | flops 805306368 | bytes 4259840 | tf_op jit(solution)/shard_map/triangular_solve | solution.py:28
  138.7 3.7 %convolution_multiply_fusion = f32[128,128]{1,0:T(8,128)S(1)} fusion(f32[4096,128]{1,0:T(8,128)S(1)} %fusion.4), kind=kOutput, calls=%fused_computation.1 | convolution fusion | flops 805322752 | bytes 2162688 | tf_op jit(solution)/shard_map/dot_general | solution.py:32
  142.4 11.7 %cholesky.56 = f32[128,128]{1,0:T(8,128)S(1)} custom-call(f32[128,128]{1,0:T(8,128)S(1)} %convolution_multiply_fusion), custom_call_target="Cholesky" | custom-call | tf_op jit(solution)/shard_map/jit(cholesky)/cholesky | solution.py:58
  154.2 0.6 compare_reduce_fusion
  154.8 1.3 select_bitcast_fusion
  156.1 9.8 %custom-call.11 = f32[1,128,128]{1,2,0:T(8,128)S(1)} custom-call(f32[1,128,128]{2,1,0:T(8,128)S(1)} %get-tuple-element.4), custom_call_target="InvertDiagBlocksLowerTriangular" | custom-call | tf_op jit(solution)/shard_map/triangular_solve | solution.py:28
  165.9 0.8 fusion.2
  (4 shorter events, 0.1 us)
Async XLA Ops:
  0.6 1.2 copy-start
  0.6 5.2 %copy-start.2 = (f32[224,4096]{1,0:T(8,128)S(1)}, f32[224,4096]{1,0:T(8,128)}, u32[]{:S(2)}) copy-start(f32[224,4096]{1,0:T(8,128)} %param.3) | copy-start | bytes 11010052
  81.7 15.7 %all-to-all-start.4 = ((f32[16,128,128]{2,1,0:T(8,128)}), f32[16,128,128]{2,1,0:T(8,128)S(1)}, u32[]{:S(2)}, u32[]{:S(2)}) async-start(f32[16,128,128]{2,1,0:T(8,128)} %broadcast_in_dim.23), calls=%async_computation.4 | async-start | bytes 2097152 | tf_op jit(solution)/shard_map/all_to_all | solution.py:11
  108.8 1.4 copy-start.1

commit v2 on v1

v2 whole, which is shorter than its diff:
```python
import functools

import jax
import jax.numpy as jnp
from jax import lax
from jax.experimental import pallas as pl
from jax.experimental.pallas import tpu as pltpu
from jax.sharding import Mesh, PartitionSpec as P

AXES = ("y", "z", "core", "x")
CHUNKS = 8
PANEL = 32
LANES = 128
F32, BF16 = jnp.float32, jnp.bfloat16
VMEM_LIMIT = 60 * 1024 * 1024


def dot(left, right, right_dim=0):
    return lax.dot_general(left, right, (((1,), (right_dim,)), ((), ())), preferred_element_type=F32)


def split(values):
    first = values.astype(BF16)
    rest = values - first.astype(F32)
    second = rest.astype(BF16)
    return first, second, (rest - second.astype(F32)).astype(BF16)


def dot_split(left, right):
    rows = left[0].shape[0]
    high = dot(jnp.concatenate(left, axis=0), right[0])
    middle = dot(jnp.concatenate(left[:2], axis=0), right[1])
    low = dot(left[0], right[2])
    small = high[2 * rows :] + middle[rows:] + low
    return high[:rows] + (high[rows : 2 * rows] + middle[:rows] + small)


def image_kernel(core_ref, emb_hbm, test_hbm, sketch_ref, keep_ref, send_ref, emb, test, terms, sems):
    rows, columns = emb.shape[1], emb.shape[2]
    copies = []
    for c in range(CHUNKS):
        span = pl.ds(c * columns, columns)
        copies.append(
            (
                pltpu.make_async_copy(emb_hbm.at[:, span], emb.at[c], sems.at[0, c]),
                pltpu.make_async_copy(test_hbm.at[span], test.at[c], sems.at[1, c]),
            )
        )
    for pair in copies:
        for copy in pair:
            copy.start()
    sketch = jnp.zeros((rows, LANES), F32)
    for c in range(CHUNKS):
        for copy in copies[c]:
            copy.wait()
        parts = split(emb[c])
        for t in range(3):
            terms[t, c] = parts[t]
        product = dot(jnp.concatenate(parts, axis=0), test[c])
        sketch += product[:rows] + (product[rows : 2 * rows] + product[2 * rows :])
    sketch_ref[...] = sketch
    left = split(sketch.T)
    per_chunk = columns // LANES
    core = core_ref[0]
    for out, half in ((send_ref, 1 - core), (keep_ref, core)):
        for i in range(CHUNKS // 2):
            c = half * (CHUNKS // 2) + i
            part = dot_split(left, [terms[t, c] for t in range(3)])
            for b in range(per_chunk):
                out[i * per_chunk + b] = part[:, b * LANES : (b + 1) * LANES]


def local_image(core, embeddings, test_matrix):
    rows, width = embeddings.shape
    columns = width // CHUNKS
    blocks = jax.ShapeDtypeStruct((width // (2 * LANES), LANES, LANES), F32)
    vmem = pl.BlockSpec(memory_space=pltpu.VMEM)
    return pl.pallas_call(
        image_kernel,
        out_shape=[jax.ShapeDtypeStruct((rows, LANES), F32), blocks, blocks],
        in_specs=[
            pl.BlockSpec(memory_space=pltpu.SMEM),
            pl.BlockSpec(memory_space=pl.ANY),
            pl.BlockSpec(memory_space=pl.ANY),
        ],
        out_specs=[vmem] * 3,
        scratch_shapes=[
            pltpu.VMEM((CHUNKS, rows, columns), F32),
            pltpu.VMEM((CHUNKS, columns, LANES), BF16),
            pltpu.VMEM((3, CHUNKS, rows, columns), BF16),
            pltpu.SemaphoreType.DMA((2, CHUNKS)),
        ],
        compiler_params=pltpu.CompilerParams(vmem_limit_bytes=VMEM_LIMIT),
        cost_estimate=pl.CostEstimate(flops=2 * 9 * rows * width * LANES, bytes_accessed=4 * rows * width, transcendentals=0),
        name="local_image",
    )(core, embeddings, test_matrix)


def over_sublanes(tile, row):
    return jnp.broadcast_to(tile[row : row + 1], tile.shape)


def over_lanes(tile, lane):
    return jnp.broadcast_to(tile[:, lane : lane + 1], tile.shape)


def eliminate(a, b, first_lane):
    sublane = lax.broadcasted_iota(jnp.int32, (8, LANES), 0)
    for g in range(len(a)):
        column = {q: [over_lanes(a[q], first_lane + 8 * g + k) for k in range(8)] for q in range(g, len(a))}
        for i in range(8):
            inverse = 1.0 / over_sublanes(column[g][i], i)
            row_a, row_b = over_sublanes(a[g], i), over_sublanes(b[g], i)
            pivots = [over_sublanes(column[g][k], i) for k in range(8)]
            for q in range(g, len(a)):
                factor = column[q][i] * inverse
                if q == g:
                    if i == 7:
                        continue
                    factor = jnp.where(sublane > i, factor, 0.0)
                for k in range(i + 1, 8):
                    column[q][k] = column[q][k] - factor * pivots[k]
                a[q] = a[q] - factor * row_a
                b[q] = b[q] - factor * row_b


def factorize(gram):
    size = gram.shape[0]
    tiles = lambda value: [value[8 * t : 8 * t + 8] for t in range(PANEL // 8)]
    row = lax.broadcasted_iota(jnp.int32, (size, size), 0)
    column = lax.broadcasted_iota(jnp.int32, (size, size), 1)
    other = jnp.where(row == column, 1.0, 0.0).astype(F32)
    uppers, inverses = [], []
    for start in range(0, size, PANEL):
        a, b = tiles(gram), tiles(other)
        eliminate(a, b, start)
        a, b = jnp.concatenate(a, axis=0), jnp.concatenate(b, axis=0)
        here = row[start : start + PANEL]
        lanes = column[start : start + PANEL]
        scale = lax.rsqrt(jnp.sum(jnp.where(here == lanes, a, 0.0), axis=1, keepdims=True))
        upper, inverse = jnp.where(lanes >= here, a * scale, 0.0), b * scale
        uppers.append(upper)
        inverses.append(inverse)
        if start + PANEL < size:
            below = split(upper.T[start + PANEL :])
            gram = gram[PANEL:] - dot_split(below, split(upper))
            other = other[PANEL:] - dot_split(below, split(inverse))
    return jnp.concatenate(uppers, axis=0), jnp.concatenate(inverses, axis=0)


def finish_kernel(
    total_rows, place_ref, mine_ref, other_ref, sketch_ref, test_ref,
    basis_ref, right_ref, factor_ref, loadings, turned,
):
    blocks = mine_ref.shape[0]
    group = 4
    core = place_ref[0]
    halves = ((mine_ref, core), (other_ref, 1 - core))

    def wide(ref, first):
        return jnp.concatenate([ref[first + b] for b in range(group)], axis=1)

    partial = []
    for ref, half in halves:
        total = jnp.zeros((LANES, LANES), F32)
        for first in range(0, blocks, group):
            terms = jnp.concatenate(split(wide(ref, first)), axis=0)
            offset = pl.multiple_of((half * blocks + first) * LANES, group * LANES)
            product = dot(terms, test_ref[pl.ds(offset, group * LANES), :])
            total += product[:LANES] + (product[LANES : 2 * LANES] + product[2 * LANES :])
        partial.append(total)
    gram = (partial[0] + partial[1]) * (0.5 / total_rows)
    _, inverse = factorize(gram + gram.T)
    left = split(inverse)

    partial = []
    for h, (ref, _) in enumerate(halves):
        total = jnp.zeros((LANES, LANES), F32)
        for first in range(0, blocks, group):
            values = dot_split(left, split(wide(ref, first)))
            for b in range(group):
                loadings[h * blocks + first + b] = values[:, b * LANES : (b + 1) * LANES]
            terms = split(values)
            product = dot(jnp.concatenate(terms, axis=0), terms[0], 1)
            cross = product[LANES : 2 * LANES] + product[2 * LANES :]
            total += product[:LANES] + (cross + cross.T + dot(terms[1], terms[1], 1))
        partial.append(total)
    upper, second = factorize((partial[0] + partial[1]) / (2 * blocks * LANES))
    factor_ref[...] = upper.T

    basis_ref[...] = dot_split(split(sketch_ref[...]), split(inverse.T))
    turned[...] = dot_split(split(second), split(loadings[place_ref[1]])).T
    right_ref[...] = turned[pl.ds(pl.multiple_of(place_ref[2], 8), right_ref.shape[0]), :]


def finish(place, mine, other, sketch, test_matrix, total_rows, own_rows):
    vmem = pl.BlockSpec(memory_space=pltpu.VMEM)
    return pl.pallas_call(
        functools.partial(finish_kernel, total_rows),
        out_shape=[
            jax.ShapeDtypeStruct(sketch.shape, F32),
            jax.ShapeDtypeStruct((own_rows, LANES), F32),
            jax.ShapeDtypeStruct((LANES, LANES), F32),
        ],
        in_specs=[pl.BlockSpec(memory_space=pltpu.SMEM)] + [vmem] * 4,
        out_specs=[vmem] * 3,
        scratch_shapes=[
            pltpu.VMEM((2 * mine.shape[0], LANES, LANES), F32),
            pltpu.VMEM((LANES, LANES), F32),
        ],
        compiler_params=pltpu.CompilerParams(vmem_limit_bytes=VMEM_LIMIT),
        name="finish",
    )(place, mine, other, sketch, test_matrix)


def exchange(values, axes):
    return lax.all_to_all(values, axes, 0, 0, tiled=False)


def scatter_sum(values, axes):
    parts = lax.axis_size(axes)
    blocks = values.reshape((parts, values.shape[0] // parts) + values.shape[1:])
    return jnp.sum(exchange(blocks, axes), axis=0)


def gather(values, axes):
    parts = lax.axis_size(axes)
    blocks = exchange(jnp.broadcast_to(values[None], (parts,) + values.shape), axes)
    return blocks.reshape((parts * values.shape[0],) + values.shape[1:])


def swap_cores(values):
    return lax.ppermute(values, "core", [(0, 1), (1, 0)])


def per_device(embeddings, test_matrix):
    devices_all = lax.axis_size(AXES)
    rows, width = embeddings.shape
    own_rows = width // devices_all
    core = lax.axis_index("core")
    sketch, keep, send = local_image(core.reshape(1), embeddings, test_matrix)
    image = keep + swap_cores(send)
    block = scatter_sum(image, ("x", "y")).reshape(LANES, LANES)
    block = gather(scatter_sum(block, "z"), "z")
    mine = gather(block[None], ("x", "y"))
    other = swap_cores(mine)
    first = lax.axis_index(AXES) * own_rows
    half_blocks = mine.shape[0]
    own_block = first // LANES
    slot = jnp.where(own_block // half_blocks == core, 0, half_blocks) + own_block % half_blocks
    place = jnp.stack([core, slot, first % LANES])
    basis, right_basis, factor = finish(place, mine, other, sketch, test_matrix, rows * devices_all, own_rows)
    return (basis, right_basis, factor)


def solution(mesh):
    fine = Mesh(mesh.devices.reshape(4, 16, 2, 4), AXES)
    return jax.shard_map(
        per_device,
        mesh=fine,
        in_specs=(P(AXES, None), P()),
        out_specs=(P(AXES, None), P(AXES, None), P()),
        check_vma=False,
    )
```

time: 167 us -> 124 us (0.74)
  other arithmetic: 47.6 us -> 2.07 us
  Pallas kernels: 0 us -> 25.8 us
  matrix products: 16.2 us -> 0 us
  starting transfers between devices: 3.73 us -> 17.3 us
  waiting for transfers between devices: 12 us -> 3.85 us
  blocking collectives: 81 us -> 73 us
  local copies, waits for them, and re-layouts: 5.35 us -> 1.14 us
    another operation x10 -> x1, other arithmetic: 46.3 us -> 0.65 us  [per_device(): place = jnp.stack([core, slot, first % LANES])]
    pallas_call x0 -> x2, Pallas kernels: none -> 25.8 us  [the longest x1 16.8 us: finish(): pl.pallas_call(functools.partial(finish_kernel, total_rows), out_shape=[j...]
    ppermute x0 -> x2, starting transfers between devices: none -> 17.3 us  [swap_cores(): return lax.ppermute(values, 'core', [(0, 1), (1, 0)])]
    all_to_all x1 -> x0, waiting for transfers between devices: 12 us -> none  [exchange(): return lax.all_to_all(values, axes, 0, 0, tiled=False)]
    dot_general x4 -> x0, matrix products: 11.2 us -> none  [dot(): lax.dot_general(left, right, (((left_dim,), (right_dim,)), ((), ())), pre...]
    all_to_all x5 -> x4, blocking collectives: 81 us -> 73 us  [exchange(): return lax.all_to_all(values, axes, 0, 0, tiled=False)]
    another operation x3 -> x0, matrix products: 5.04 us -> none  [lower_solve(): lax.linalg.triangular_solve(lower, values, left_side=False, lower=True, t...]
    ppermute x0 -> x2, waiting for transfers between devices: none -> 3.85 us  [swap_cores(): return lax.ppermute(values, 'core', [(0, 1), (1, 0)])]
  transfers between devices with their start and end apart: 1 -> 2, of which waited for: 1 -> 2; matrix products, arithmetic and copies ran while one was open for 0% -> 1% of each run, Pallas kernels for 0% -> 0%
where the time goes in v2:
time: 124 us
  blocking collectives  73 us (59%)
  Pallas kernels  25.8 us (21%)
  starting transfers between devices  17.3 us (14%)
  waiting for transfers between devices  3.85 us (3%)
  other arithmetic  2.07 us (2%)
    all_to_all x4, blocking collectives, exchange(): return lax.all_to_all(values, axes, 0, 0, tiled=False)  73 us
    ppermute x2, starting transfers between devices, swap_cores(): return lax.ppermute(values, 'core', [(0, 1), (1, 0)])  17.3 us
    pallas_call x1, Pallas kernels, finish(): pl.pallas_call(functools.partial(finish_kernel, total_rows), out_shape=[j...  16.8 us
    pallas_call x1, Pallas kernels, local_image(): pl.pallas_call(image_kernel, out_shape=[jax.ShapeDtypeStruct((rows, LANES...  9 us
    ppermute x2, waiting for transfers between devices, swap_cores(): return lax.ppermute(values, 'core', [(0, 1), (1, 0)])  3.85 us
  transfers between devices with their start and end apart: 2, of which 2 were waited for; matrix products, arithmetic and copies ran while one was open for 1% of the time, Pallas kernels for 0%

profile of v2, /device:TPU:1, one launch (start us, length us, event | category | flops | bytes accessed | tf_op | source)
XLA Modules:
  0.0 123.8 jit_solution(13560037707468306132)
XLA Ops:
  0.6 9.0 %local_image.1 = (f32[224,128]{1,0:T(8,128)}, f32[16,128,128]{2,1,0:T(8,128)}, f32[16,128,128]{2,1,0:T(8,128)}) custom-call(s32[1]{0:T(128)} %bitcast.core_ref, f32[224,4096]{1,0:T(8,128)} %emb_hbm.1, bf16[4096,128]{1,0:T(8,128)(2,1)} %test_ref.1), custom_call_target="tpu_custom_call" | custom-call | flops 2113929216 | bytes 3670016 | tf_op jit(solution)/shard_map/local_image/pallas_call | solution.py:78
  9.6 8.8 %collective-permute-start = (f32[16,128,128]{2,1,0:T(8,128)}, f32[16,128,128]{2,1,0:T(8,128)S(1)}, u32[]{:S(2)}, u32[]{:S(2)}) collective-permute-start(f32[16,128,128]{2,1,0:T(8,128)} %get-tuple-element.7), channel_id=1, source_target_pairs={{0,4},{4,0},{1,5},{5,1},{2,6},{6,2},{3,7},{7,3},{8,12},{12,8},{9,1... | collective-permute-start | bytes 3145736 | tf_op jit(solution)/shard_map/ppermute | solution.py:233
  18.4 2.5 %collective-permute-done = f32[16,128,128]{2,1,0:T(8,128)S(1)} collective-permute-done((f32[16,128,128]{2,1,0:T(8,128)}, f32[16,128,128]{2,1,0:T(8,128)S(1)}, u32[]{:S(2)}, u32[]{:S(2)}) %collective-permute-start) | collective-permute-done | bytes 1048608 | tf_op jit(solution)/shard_map/ppermute | solution.py:233
  20.9 1.3 %add_bitcast_fusion = f32[16,1,128,128]{3,2,1,0:T(8,128)S(1)} fusion(f32[16,128,128]{2,1,0:T(8,128)} %get-tuple-element.6, f32[16,128,128]{2,1,0:T(8,128)S(1)} %collective-permute-done), kind=kLoop, calls=%fused_computation | loop fusion | flops 262144 | bytes 3145728 | tf_op jit(solution)/shard_map/reshape | solution.py:222
  22.3 18.5 %all_to_all.20 = f32[16,1,128,128]{3,2,1,0:T(8,128)S(1)} all-to-all(f32[16,1,128,128]{3,2,1,0:T(8,128)S(1)} %add_bitcast_fusion), channel_id=1, replica_groups=mesh['y'=4,'z'=16,'core'=2,'x'=4] {'x','y'}, dimensions={0} | all-to-all | bytes 2097152 | tf_op jit(solution)/shard_map/all_to_all | solution.py:217
  40.8 0.1 reduce_sum.18
  40.8 25.0 %all_to_all.21 = f32[16,8,128]{2,1,0:T(8,128)S(1)} all-to-all(f32[16,8,128]{2,1,0:T(8,128)S(1)} %bitcast.12), channel_id=1, replica_groups=mesh['y'=4,'z'=16,'core'=2,'x'=4] {'z'}, dimensions={0} | all-to-all | bytes 131072 | tf_op jit(solution)/shard_map/all_to_all | solution.py:217
  65.9 14.3 %all_to_all.22 = f32[16,8,128]{2,1,0:T(8,128)S(1)} all-to-all(f32[16,8,128]{2,1,0:T(8,128)S(1)} %broadcast_in_dim.6), channel_id=1, replica_groups=mesh['y'=4,'z'=16,'core'=2,'x'=4] {'z'}, dimensions={0} | all-to-all | bytes 131072 | tf_op jit(solution)/shard_map/all_to_all | solution.py:217
  80.2 0.1 broadcast_in_dim.15
  80.3 15.2 %all_to_all.23 = f32[16,1,128,128]{3,2,1,0:T(8,128)S(1)} all-to-all(f32[16,1,128,128]{3,2,1,0:T(8,128)S(1)} %broadcast_in_dim.15), channel_id=1, replica_groups=mesh['y'=4,'z'=16,'core'=2,'x'=4] {'x','y'}, dimensions={0} | all-to-all | bytes 2097152 | tf_op jit(solution)/shard_map/all_to_all | solution.py:217
  95.5 0.0 copy-start
  95.5 8.5 %collective-permute-start.1 = (f32[16,128,128]{2,1,0:T(8,128)S(1)}, f32[16,128,128]{2,1,0:T(8,128)S(1)}, u32[]{:S(2)}, u32[]{:S(2)}) collective-permute-start(f32[16,128,128]{2,1,0:T(8,128)S(1)} %bitcast.10), channel_id=1, source_target_pairs={{0,4},{4,0},{1,5},{5,1},{2,6},{6,2},{3,7},{7,3},{8,12},{12,8},{9,1... | collective-permute-start | bytes 3145736 | tf_op jit(solution)/shard_map/ppermute | solution.py:233
  104.0 0.7 pad_add_fusion.place_ref
  104.7 1.4 %collective-permute-done.1.other_ref = f32[16,128,128]{2,1,0:T(8,128)S(1)} collective-permute-done((f32[16,128,128]{2,1,0:T(8,128)S(1)}, f32[16,128,128]{2,1,0:T(8,128)S(1)}, u32[]{:S(2)}, u32[]{:S(2)}) %collective-permute-start.1) | collective-permute-done | bytes 1048608 | tf_op jit(solution)/shard_map/ppermute | solution.py:233
  106.1 0.0 copy-start.1
  106.1 0.0 copy-done
  106.1 1.0 copy-done.1
  107.1 16.8 %finish.1 = (f32[224,128]{1,0:T(8,128)}, f32[8,128]{1,0:T(8,128)}, f32[128,128]{1,0:T(8,128)}) custom-call(s32[3]{0:T(128)} %pad_add_fusion.place_ref, f32[16,128,128]{2,1,0:T(8,128)} %bitcast.11, f32[16,128,128]{2,1,0:T(8,128)} %copy-done.1, f32[224,128]{1,0:T(8,128)} %get-tuple-element.8.sketch_ref, bf16[4096,128]{1,0:T(8,128)(2,1)} %test_ref.1), custom_call_target="tpu_custom_call" | custom-call | tf_op jit(solution)/shard_map/finish/pallas_call | solution.py:198
  (2 shorter events, 0.0 us)
Async XLA Ops:
  9.6 11.3 %collective-permute-start = (f32[16,128,128]{2,1,0:T(8,128)}, f32[16,128,128]{2,1,0:T(8,128)S(1)}, u32[]{:S(2)}, u32[]{:S(2)}) collective-permute-start(f32[16,128,128]{2,1,0:T(8,128)} %get-tuple-element.7), channel_id=1, source_target_pairs={{0,4},{4,0},{1,5},{5,1},{2,6},{6,2},{3,7},{7,3},{8,12},{12,8},{9,1... | collective-permute-start | bytes 3145736 | tf_op jit(solution)/shard_map/ppermute | solution.py:233
  95.5 10.6 %copy-start = (f32[16,1,128,128]{3,2,1,0:T(8,128)}, f32[16,1,128,128]{3,2,1,0:T(8,128)S(1)}, u32[]{:S(2)}) copy-start(f32[16,1,128,128]{3,2,1,0:T(8,128)S(1)} %all_to_all.23) | copy-start | bytes 3145732
  95.5 10.6 %collective-permute-start.1 = (f32[16,128,128]{2,1,0:T(8,128)S(1)}, f32[16,128,128]{2,1,0:T(8,128)S(1)}, u32[]{:S(2)}, u32[]{:S(2)}) collective-permute-start(f32[16,128,128]{2,1,0:T(8,128)S(1)} %bitcast.10), channel_id=1, source_target_pairs={{0,4},{4,0},{1,5},{5,1},{2,6},{6,2},{3,7},{7,3},{8,12},{12,8},{9,1... | collective-permute-start | bytes 3145736 | tf_op jit(solution)/shard_map/ppermute | solution.py:233
  106.1 1.0 copy-start.1

commit v3 on v2

--- a/solution.py
+++ b/solution.py
@@ -8,11 +8,12 @@
 from jax.sharding import Mesh, PartitionSpec as P
 
 AXES = ("y", "z", "core", "x")
-CHUNKS = 8
+CHUNKS = 4
+STEP = 512
 PANEL = 32
 LANES = 128
 F32, BF16 = jnp.float32, jnp.bfloat16
-VMEM_LIMIT = 60 * 1024 * 1024
+VMEM_LIMIT = 24 * 1024 * 1024
 
 
 def dot(left, right, right_dim=0):
@@ -35,15 +36,27 @@
     return high[:rows] + (high[rows : 2 * rows] + middle[:rows] + small)
 
 
-def image_kernel(core_ref, emb_hbm, test_hbm, sketch_ref, keep_ref, send_ref, emb, test, terms, sems):
-    rows, columns = emb.shape[1], emb.shape[2]
+def image_blocks(left, right, out, first):
+    part = dot(left[0], right[0]) + (
+        (dot(left[1], right[0]) + dot(left[0], right[1]))
+        + (dot(left[2], right[0]) + dot(left[1], right[1]) + dot(left[0], right[2]))
+    )
+    for b in range(part.shape[1] // LANES):
+        out[first + b] = part[:, b * LANES : (b + 1) * LANES]
+
+
+def sketch_kernel(core_ref, emb_hbm, test_hbm, sketch_ref, send_ref, keep_terms, emb, test, send_terms, sems):
+    rows, width = emb.shape
+    columns = width // CHUNKS
+    core = core_ref[0]
     copies = []
     for c in range(CHUNKS):
-        span = pl.ds(c * columns, columns)
+        there = pl.multiple_of(lax.rem(core * (width // 2) + c * columns, width), columns)
+        here = pl.ds(c * columns, columns)
         copies.append(
             (
-                pltpu.make_async_copy(emb_hbm.at[:, span], emb.at[c], sems.at[0, c]),
-                pltpu.make_async_copy(test_hbm.at[span], test.at[c], sems.at[1, c]),
+                pltpu.make_async_copy(emb_hbm.at[:, pl.ds(there, columns)], emb.at[:, here], sems.at[0, c]),
+                pltpu.make_async_copy(test_hbm.at[pl.ds(there, columns)], test.at[here], sems.at[1, c]),
             )
         )
     for pair in copies:
@@ -53,47 +66,69 @@
     for c in range(CHUNKS):
         for copy in copies[c]:
             copy.wait()
-        parts = split(emb[c])
+        here = slice(c * columns, (c + 1) * columns)
+        parts = split(emb[:, here])
+        terms, first = (keep_terms, 0) if c < CHUNKS // 2 else (send_terms, width // 2)
         for t in range(3):
-            terms[t, c] = parts[t]
-        product = dot(jnp.concatenate(parts, axis=0), test[c])
-        sketch += product[:rows] + (product[rows : 2 * rows] + product[2 * rows :])
+            terms[t, :, here.start - first : here.stop - first] = parts[t]
+            sketch += dot(parts[t], test[here])
     sketch_ref[...] = sketch
     left = split(sketch.T)
-    per_chunk = columns // LANES
-    core = core_ref[0]
-    for out, half in ((send_ref, 1 - core), (keep_ref, core)):
-        for i in range(CHUNKS // 2):
-            c = half * (CHUNKS // 2) + i
-            part = dot_split(left, [terms[t, c] for t in range(3)])
-            for b in range(per_chunk):
-                out[i * per_chunk + b] = part[:, b * LANES : (b + 1) * LANES]
-
-
-def local_image(core, embeddings, test_matrix):
+    for start in range(0, width // 2, STEP):
+        image_blocks(left, [send_terms[t, :, start : start + STEP] for t in range(3)], send_ref, start // LANES)
+
+
+def keep_kernel(sketch_ref, keep_terms, keep_ref):
+    left = split(sketch_ref[...].T)
+    for start in range(0, keep_terms.shape[2], STEP):
+        image_blocks(left, [keep_terms[t, :, start : start + STEP] for t in range(3)], keep_ref, start // LANES)
+
+
+def local_sketch(core, embeddings, test_matrix):
     rows, width = embeddings.shape
-    columns = width // CHUNKS
-    blocks = jax.ShapeDtypeStruct((width // (2 * LANES), LANES, LANES), F32)
+    half = width // 2
     vmem = pl.BlockSpec(memory_space=pltpu.VMEM)
     return pl.pallas_call(
-        image_kernel,
-        out_shape=[jax.ShapeDtypeStruct((rows, LANES), F32), blocks, blocks],
+        sketch_kernel,
+        out_shape=[
+            pltpu.VMEM((rows, LANES), F32),
+            pltpu.VMEM((half // LANES, LANES, LANES), F32),
+            pltpu.VMEM((3, rows, half), BF16),
+        ],
         in_specs=[
             pl.BlockSpec(memory_space=pltpu.SMEM),
-            pl.BlockSpec(memory_space=pl.ANY),
-            pl.BlockSpec(memory_space=pl.ANY),
+            pl.BlockSpec(memory_space=pltpu.HBM),
+            pl.BlockSpec(memory_space=pltpu.HBM),
         ],
         out_specs=[vmem] * 3,
         scratch_shapes=[
-            pltpu.VMEM((CHUNKS, rows, columns), F32),
-            pltpu.VMEM((CHUNKS, columns, LANES), BF16),
-            pltpu.VMEM((3, CHUNKS, rows, columns), BF16),
+            pltpu.VMEM((rows, width), F32),
+            pltpu.VMEM((width, LANES), BF16),
+            pltpu.VMEM((3, rows, half), BF16),
             pltpu.SemaphoreType.DMA((2, CHUNKS)),
         ],
         compiler_params=pltpu.CompilerParams(vmem_limit_bytes=VMEM_LIMIT),
-        cost_estimate=pl.CostEstimate(flops=2 * 9 * rows * width * LANES, bytes_accessed=4 * rows * width, transcendentals=0),
-        name="local_image",
-    )(core, embeddings, test_matrix)
+        cost_estimate=pl.CostEstimate(flops=12 * rows * width * LANES, bytes_accessed=4 * rows * width, transcendentals=0),
+        name="local_sketch",
+    )(
+        core,
+        pltpu.with_memory_space_constraint(embeddings, pltpu.HBM),
+        pltpu.with_memory_space_constraint(test_matrix, pltpu.HBM),
+    )
+
+
+def keep_image(sketch, keep_terms):
+    rows, half = keep_terms.shape[1:]
+    vmem = pl.BlockSpec(memory_space=pltpu.VMEM)
+    return pl.pallas_call(
+        keep_kernel,
+        out_shape=pltpu.VMEM((half // LANES, LANES, LANES), F32),
+        in_specs=[vmem] * 2,
+        out_specs=vmem,
+        compiler_params=pltpu.CompilerParams(vmem_limit_bytes=VMEM_LIMIT),
+        cost_estimate=pl.CostEstimate(flops=12 * rows * half * LANES, bytes_accessed=6 * rows * half, transcendentals=0),
+        name="keep_image",
+    )(sketch, keep_terms)
 
 
 def over_sublanes(tile, row):
@@ -238,8 +273,9 @@
     rows, width = embeddings.shape
     own_rows = width // devices_all
     core = lax.axis_index("core")
-    sketch, keep, send = local_image(core.reshape(1), embeddings, test_matrix)
-    image = keep + swap_cores(send)
+    sketch, send, keep_terms = local_sketch(core.reshape(1), embeddings, test_matrix)
+    arriving = swap_cores(send)
+    image = keep_image(sketch, keep_terms) + arriving
     block = scatter_sum(image, ("x", "y")).reshape(LANES, LANES)
     block = gather(scatter_sum(block, "z"), "z")
     mine = gather(block[None], ("x", "y"))

time: 124 us -> 116 us (0.935)
  Pallas kernels: 25.8 us -> 20.9 us
  other arithmetic: 2.07 us -> 0.3 us
    pallas_call x1 -> x2, Pallas kernels: 9 us -> 5.51 us  [the longest x1 4.49 us: local_sketch(): pl.pallas_call(sketch_kernel, out_shape=[pltpu.VMEM((rows, LANES), F32),...]
    pallas_call x1, Pallas kernels: 16.8 us -> 15.4 us  [finish(): pl.pallas_call(functools.partial(finish_kernel, total_rows), out_shape=[j...]
  transfers between devices with their start and end apart: 2 -> 2, of which waited for: 2 -> 2; matrix products, arithmetic and copies ran while one was open for 1% -> 0% of each run, Pallas kernels for 0% -> 1%
where the time goes in v3:
time: 116 us
  blocking collectives  73.2 us (63%)
  Pallas kernels  20.9 us (18%)
  starting transfers between devices  17.3 us (15%)
  waiting for transfers between devices  3.18 us (3%)
    all_to_all x4, blocking collectives, exchange(): return lax.all_to_all(values, axes, 0, 0, tiled=False)  73.2 us
    ppermute x2, starting transfers between devices, swap_cores(): return lax.ppermute(values, 'core', [(0, 1), (1, 0)])  17.3 us
    pallas_call x1, Pallas kernels, finish(): pl.pallas_call(functools.partial(finish_kernel, total_rows), out_shape=[j...  15.4 us
    pallas_call x1, Pallas kernels, local_sketch(): pl.pallas_call(sketch_kernel, out_shape=[pltpu.VMEM((rows, LANES), F32),...  4.49 us
    ppermute x2, waiting for transfers between devices, swap_cores(): return lax.ppermute(values, 'core', [(0, 1), (1, 0)])  3.18 us
  transfers between devices with their start and end apart: 2, of which 2 were waited for; matrix products, arithmetic and copies ran while one was open for 0% of the time, Pallas kernels for 1%

profile of v3, /device:TPU:1, one launch (start us, length us, event | category | flops | bytes accessed | tf_op | source)
XLA Modules:
  0.0 115.7 jit_solution(3273755304843306072)
XLA Ops:
  0.6 4.5 %local_sketch.1 = (f32[224,128]{1,0:T(8,128)S(1)}, f32[16,128,128]{2,1,0:T(8,128)S(1)}, bf16[3,224,2048]{2,1,0:T(8,128)(2,1)S(1)}) custom-call(s32[1]{0:T(128)} %bitcast.core_ref, f32[224,4096]{1,0:T(8,128)} %emb_hbm.1, bf16[4096,128]{1,0:T(8,128)(2,1)} %test_ref.1), custom_call_target="tpu_custom_call" | custom-call | flops 1409286144 | bytes 3670016 | tf_op jit(solution)/shard_map/local_sketch/pallas_call | solution.py:91
  5.1 8.8 %collective-permute-start = (f32[16,128,128]{2,1,0:T(8,128)S(1)}, f32[16,128,128]{2,1,0:T(8,128)S(1)}, u32[]{:S(2)}, u32[]{:S(2)}) collective-permute-start(f32[16,128,128]{2,1,0:T(8,128)S(1)} %get-tuple-element.8), channel_id=1, source_target_pairs={{0,4},{4,0},{1,5},{5,1},{2,6},{6,2},{3,7},{7,3},{8,12},{12,8},{9,1... | collective-permute-start | bytes 3145736 | tf_op jit(solution)/shard_map/ppermute | solution.py:268
  13.9 1.0 keep_image.1
  15.0 1.2 %collective-permute-done = f32[16,128,128]{2,1,0:T(8,128)S(1)} collective-permute-done((f32[16,128,128]{2,1,0:T(8,128)S(1)}, f32[16,128,128]{2,1,0:T(8,128)S(1)}, u32[]{:S(2)}, u32[]{:S(2)}) %collective-permute-start) | collective-permute-done | bytes 1048608 | tf_op jit(solution)/shard_map/ppermute | solution.py:268
  16.2 0.2 add_bitcast_fusion
  16.3 0.0 copy-start
  16.4 18.6 %all_to_all.20 = f32[16,1,128,128]{3,2,1,0:T(8,128)S(1)} all-to-all(f32[16,1,128,128]{3,2,1,0:T(8,128)S(1)} %add_bitcast_fusion), channel_id=1, replica_groups=mesh['y'=4,'z'=16,'core'=2,'x'=4] {'x','y'}, dimensions={0} | all-to-all | bytes 2097152 | tf_op jit(solution)/shard_map/all_to_all | solution.py:252
  35.0 0.1 reduce_sum.18
  35.0 25.0 %all_to_all.21 = f32[16,8,128]{2,1,0:T(8,128)S(1)} all-to-all(f32[16,8,128]{2,1,0:T(8,128)S(1)} %bitcast.12), channel_id=1, replica_groups=mesh['y'=4,'z'=16,'core'=2,'x'=4] {'z'}, dimensions={0} | all-to-all | bytes 131072 | tf_op jit(solution)/shard_map/all_to_all | solution.py:252
  60.1 14.3 %all_to_all.22 = f32[16,8,128]{2,1,0:T(8,128)S(1)} all-to-all(f32[16,8,128]{2,1,0:T(8,128)S(1)} %broadcast_in_dim.6), channel_id=1, replica_groups=mesh['y'=4,'z'=16,'core'=2,'x'=4] {'z'}, dimensions={0} | all-to-all | bytes 131072 | tf_op jit(solution)/shard_map/all_to_all | solution.py:252
  74.4 0.1 broadcast_in_dim.15
  74.5 15.2 %all_to_all.23 = f32[16,1,128,128]{3,2,1,0:T(8,128)S(1)} all-to-all(f32[16,1,128,128]{3,2,1,0:T(8,128)S(1)} %broadcast_in_dim.15), channel_id=1, replica_groups=mesh['y'=4,'z'=16,'core'=2,'x'=4] {'x','y'}, dimensions={0} | all-to-all | bytes 2097152 | tf_op jit(solution)/shard_map/all_to_all | solution.py:252
  89.7 8.5 %collective-permute-start.1 = (f32[16,128,128]{2,1,0:T(8,128)S(1)}, f32[16,128,128]{2,1,0:T(8,128)S(1)}, u32[]{:S(2)}, u32[]{:S(2)}) collective-permute-start(f32[16,128,128]{2,1,0:T(8,128)S(1)} %bitcast.10), channel_id=1, source_target_pairs={{0,4},{4,0},{1,5},{5,1},{2,6},{6,2},{3,7},{7,3},{8,12},{12,8},{9,1... | collective-permute-start | bytes 3145736 | tf_op jit(solution)/shard_map/ppermute | solution.py:268
  98.3 0.1 pad_add_fusion.place_ref
  98.3 1.9 %collective-permute-done.1.other_ref = f32[16,128,128]{2,1,0:T(8,128)S(1)} collective-permute-done((f32[16,128,128]{2,1,0:T(8,128)S(1)}, f32[16,128,128]{2,1,0:T(8,128)S(1)}, u32[]{:S(2)}, u32[]{:S(2)}) %collective-permute-start.1) | collective-permute-done | bytes 1048608 | tf_op jit(solution)/shard_map/ppermute | solution.py:268
  100.3 0.0 copy-done
  100.3 15.4 %finish.1 = (f32[224,128]{1,0:T(8,128)}, f32[8,128]{1,0:T(8,128)}, f32[128,128]{1,0:T(8,128)}) custom-call(s32[3]{0:T(128)S(1)} %pad_add_fusion.place_ref, f32[16,128,128]{2,1,0:T(8,128)S(1)} %bitcast.11, f32[16,128,128]{2,1,0:T(8,128)S(1)} %collective-permute-done.1.other_ref, f32[224,128]{1,0:T(8,128)S(1)} %get-tuple-element.6.sketch_ref, ...), custom_call_target="tpu_custom_call" | custom-call | tf_op jit(solution)/shard_map/finish/pallas_call | solution.py:233
  (2 shorter events, 0.0 us)
Async XLA Ops:
  5.1 11.1 %collective-permute-start = (f32[16,128,128]{2,1,0:T(8,128)S(1)}, f32[16,128,128]{2,1,0:T(8,128)S(1)}, u32[]{:S(2)}, u32[]{:S(2)}) collective-permute-start(f32[16,128,128]{2,1,0:T(8,128)S(1)} %get-tuple-element.8), channel_id=1, source_target_pairs={{0,4},{4,0},{1,5},{5,1},{2,6},{6,2},{3,7},{7,3},{8,12},{12,8},{9,1... | collective-permute-start | bytes 3145736 | tf_op jit(solution)/shard_map/ppermute | solution.py:268
  16.3 83.9 %copy-start = (bf16[4096,128]{1,0:T(8,128)(2,1)S(1)}, bf16[4096,128]{1,0:T(8,128)(2,1)}, u32[]{:S(2)}) copy-start(bf16[4096,128]{1,0:T(8,128)(2,1)} %test_ref.1) | copy-start | bytes 3145732
  89.7 10.6 %collective-permute-start.1 = (f32[16,128,128]{2,1,0:T(8,128)S(1)}, f32[16,128,128]{2,1,0:T(8,128)S(1)}, u32[]{:S(2)}, u32[]{:S(2)}) collective-permute-start(f32[16,128,128]{2,1,0:T(8,128)S(1)} %bitcast.10), channel_id=1, source_target_pairs={{0,4},{4,0},{1,5},{5,1},{2,6},{6,2},{3,7},{7,3},{8,12},{12,8},{9,1... | collective-permute-start | bytes 3145736 | tf_op jit(solution)/shard_map/ppermute | solution.py:268

commit v4 on v3

--- a/solution.py
+++ b/solution.py
@@ -7,7 +7,8 @@
 from jax.experimental.pallas import tpu as pltpu
 from jax.sharding import Mesh, PartitionSpec as P
 
-AXES = ("y", "z", "core", "x")
+AXES = ("y", "z_pair", "z_in_pair", "core", "x")
+NEAR = ("x", "y", "z_in_pair")
 CHUNKS = 4
 STEP = 512
 PANEL = 32
@@ -27,13 +28,11 @@
     return first, second, (rest - second.astype(F32)).astype(BF16)
 
 
-def dot_split(left, right):
-    rows = left[0].shape[0]
-    high = dot(jnp.concatenate(left, axis=0), right[0])
-    middle = dot(jnp.concatenate(left[:2], axis=0), right[1])
-    low = dot(left[0], right[2])
-    small = high[2 * rows :] + middle[rows:] + low
-    return high[:rows] + (high[rows : 2 * rows] + middle[:rows] + small)
+def dot_split(left, right, right_dim=0):
+    return dot(left[0], right[0], right_dim) + (
+        (dot(left[1], right[0], right_dim) + dot(left[0], right[1], right_dim))
+        + (dot(left[2], right[0], right_dim) + dot(left[1], right[1], right_dim) + dot(left[0], right[2], right_dim))
+    )
 
 
 def image_blocks(left, right, out, first):
@@ -141,22 +140,25 @@
 
 def eliminate(a, b, first_lane):
     sublane = lax.broadcasted_iota(jnp.int32, (8, LANES), 0)
-    for g in range(len(a)):
-        column = {q: [over_lanes(a[q], first_lane + 8 * g + k) for k in range(8)] for q in range(g, len(a))}
+    tiles = range(len(a))
+    column = {q: [over_lanes(a[q], first_lane + k) for k in range(8)] for q in tiles}
+    for g in tiles:
+        if g + 1 < len(a):
+            for q in tiles[g:]:
+                column[q] = column[q] + [over_lanes(a[q], first_lane + 8 * g + k) for k in range(8, 16)]
         for i in range(8):
-            inverse = 1.0 / over_sublanes(column[g][i], i)
+            pivots = [over_sublanes(values, i) for values in column[g]]
+            inverse = 1.0 / pivots[i]
             row_a, row_b = over_sublanes(a[g], i), over_sublanes(b[g], i)
-            pivots = [over_sublanes(column[g][k], i) for k in range(8)]
-            for q in range(g, len(a)):
+            for q in tiles[g:]:
                 factor = column[q][i] * inverse
+                for k in range(i + 1, len(pivots)):
+                    column[q][k] = column[q][k] - factor * pivots[k]
                 if q == g:
-                    if i == 7:
-                        continue
                     factor = jnp.where(sublane > i, factor, 0.0)
-                for k in range(i + 1, 8):
-                    column[q][k] = column[q][k] - factor * pivots[k]
                 a[q] = a[q] - factor * row_a
                 b[q] = b[q] - factor * row_b
+        column = {q: column[q][8:] for q in tiles[g + 1 :]}
 
 
 def factorize(gram):
@@ -178,8 +180,8 @@
         inverses.append(inverse)
         if start + PANEL < size:
             below = split(upper.T[start + PANEL :])
-            gram = gram[PANEL:] - dot_split(below, split(upper))
-            other = other[PANEL:] - dot_split(below, split(inverse))
+            change = dot_split(below, split(jnp.concatenate([upper, inverse], axis=1)))
+            gram, other = gram[PANEL:] - change[:, :size], other[PANEL:] - change[:, size:]
     return jnp.concatenate(uppers, axis=0), jnp.concatenate(inverses, axis=0)
 
 
@@ -188,7 +190,7 @@
     basis_ref, right_ref, factor_ref, loadings, turned,
 ):
     blocks = mine_ref.shape[0]
-    group = 4
+    group = 16
     core = place_ref[0]
     halves = ((mine_ref, core), (other_ref, 1 - core))
 
@@ -199,10 +201,10 @@
     for ref, half in halves:
         total = jnp.zeros((LANES, LANES), F32)
         for first in range(0, blocks, group):
-            terms = jnp.concatenate(split(wide(ref, first)), axis=0)
+            terms = split(wide(ref, first))
             offset = pl.multiple_of((half * blocks + first) * LANES, group * LANES)
-            product = dot(terms, test_ref[pl.ds(offset, group * LANES), :])
-            total += product[:LANES] + (product[LANES : 2 * LANES] + product[2 * LANES :])
+            test = test_ref[pl.ds(offset, group * LANES), :]
+            total += dot(terms[0], test) + (dot(terms[1], test) + dot(terms[2], test))
         partial.append(total)
     gram = (partial[0] + partial[1]) * (0.5 / total_rows)
     _, inverse = factorize(gram + gram.T)
@@ -210,20 +212,20 @@
 
     partial = []
     for h, (ref, _) in enumerate(halves):
-        total = jnp.zeros((LANES, LANES), F32)
+        total, cross, small = (jnp.zeros((LANES, LANES), F32) for _ in range(3))
         for first in range(0, blocks, group):
             values = dot_split(left, split(wide(ref, first)))
             for b in range(group):
                 loadings[h * blocks + first + b] = values[:, b * LANES : (b + 1) * LANES]
             terms = split(values)
-            product = dot(jnp.concatenate(terms, axis=0), terms[0], 1)
-            cross = product[LANES : 2 * LANES] + product[2 * LANES :]
-            total += product[:LANES] + (cross + cross.T + dot(terms[1], terms[1], 1))
-        partial.append(total)
+            total += dot(terms[0], terms[0], 1)
+            cross += dot(terms[1], terms[0], 1) + dot(terms[2], terms[0], 1)
+            small += dot(terms[1], terms[1], 1)
+        partial.append(total + (cross + cross.T + small))
     upper, second = factorize((partial[0] + partial[1]) / (2 * blocks * LANES))
     factor_ref[...] = upper.T
 
-    basis_ref[...] = dot_split(split(sketch_ref[...]), split(inverse.T))
+    basis_ref[...] = dot_split(split(sketch_ref[...]), left, 1)
     turned[...] = dot_split(split(second), split(loadings[place_ref[1]])).T
     right_ref[...] = turned[pl.ds(pl.multiple_of(place_ref[2], 8), right_ref.shape[0]), :]
 
@@ -258,10 +260,8 @@
     return jnp.sum(exchange(blocks, axes), axis=0)
 
 
-def gather(values, axes):
-    parts = lax.axis_size(axes)
-    blocks = exchange(jnp.broadcast_to(values[None], (parts,) + values.shape), axes)
-    return blocks.reshape((parts * values.shape[0],) + values.shape[1:])
+def copies(values, axes):
+    return exchange(jnp.broadcast_to(values[None], (lax.axis_size(axes),) + values.shape), axes)
 
 
 def swap_cores(values):
@@ -276,9 +276,9 @@
     sketch, send, keep_terms = local_sketch(core.reshape(1), embeddings, test_matrix)
     arriving = swap_cores(send)
     image = keep_image(sketch, keep_terms) + arriving
-    block = scatter_sum(image, ("x", "y")).reshape(LANES, LANES)
-    block = gather(scatter_sum(block, "z"), "z")
-    mine = gather(block[None], ("x", "y"))
+    piece = scatter_sum(image.reshape(-1, LANES), NEAR)
+    piece = jnp.sum(copies(piece, "z_pair"), axis=0)
+    mine = copies(piece, NEAR).reshape(image.shape)
     other = swap_cores(mine)
     first = lax.axis_index(AXES) * own_rows
     half_blocks = mine.shape[0]
@@ -290,7 +290,7 @@
 
 
 def solution(mesh):
-    fine = Mesh(mesh.devices.reshape(4, 16, 2, 4), AXES)
+    fine = Mesh(mesh.devices.reshape(4, 8, 2, 2, 4), AXES)
     return jax.shard_map(
         per_device,
         mesh=fine,

time: 116 us -> 108 us (0.931)
  starting transfers between devices: 17.3 us -> 13.6 us
  Pallas kernels: 20.9 us -> 18.1 us
  blocking collectives: 73.2 us -> 71.4 us
    ppermute x2, starting transfers between devices: 17.3 us -> 13.6 us  [swap_cores(): return lax.ppermute(values, 'core', [(0, 1), (1, 0)])]
    pallas_call x1, Pallas kernels: 15.4 us -> 12.6 us  [finish(): pl.pallas_call(functools.partial(finish_kernel, total_rows), out_shape=[j...]
    all_to_all x4 -> x3, blocking collectives: 73.2 us -> 71.4 us  [exchange(): return lax.all_to_all(values, axes, 0, 0, tiled=False)]
where the time goes in v4:
time: 108 us; the launch traced here: 107 us
  blocking collectives  71.4 us (66%)
  Pallas kernels  18.1 us (17%)
  starting transfers between devices  13.6 us (13%)
  waiting for transfers between devices  3.17 us (3%)
    all_to_all x3, blocking collectives, exchange(): return lax.all_to_all(values, axes, 0, 0, tiled=False)  71.4 us
    ppermute x2, starting transfers between devices, swap_cores(): return lax.ppermute(values, 'core', [(0, 1), (1, 0)])  13.6 us
    pallas_call x1, Pallas kernels, finish(): pl.pallas_call(functools.partial(finish_kernel, total_rows), out_shape=[j...  12.6 us
    pallas_call x1, Pallas kernels, local_sketch(): pl.pallas_call(sketch_kernel, out_shape=[pltpu.VMEM((rows, LANES), F32),...  4.49 us
    ppermute x2, waiting for transfers between devices, swap_cores(): return lax.ppermute(values, 'core', [(0, 1), (1, 0)])  3.17 us
  transfers between devices with their start and end apart: 2, of which 2 were waited for; matrix products, arithmetic and copies ran while one was open for 0% of the time, Pallas kernels for 1%

profile of v4, /device:TPU:1, one launch (start us, length us, event | category | flops | bytes accessed | tf_op | source)
XLA Modules:
  0.0 107.5 jit_solution(401191715783558474)
XLA Ops:
  0.6 4.5 %local_sketch.1 = (f32[224,128]{1,0:T(8,128)S(1)}, f32[16,128,128]{2,1,0:T(8,128)S(1)}, bf16[3,224,2048]{2,1,0:T(8,128)(2,1)S(1)}) custom-call(s32[1]{0:T(128)} %bitcast.core_ref, f32[224,4096]{1,0:T(8,128)} %emb_hbm.1, bf16[4096,128]{1,0:T(8,128)(2,1)} %test_ref.1), custom_call_target="tpu_custom_call" | custom-call | flops 1409286144 | bytes 3670016 | tf_op jit(solution)/shard_map/local_sketch/pallas_call | solution.py:90
  5.1 8.8 %collective-permute-start = (f32[16,128,128]{2,1,0:T(8,128)S(1)}, f32[16,128,128]{2,1,0:T(8,128)S(1)}, u32[]{:S(2)}, u32[]{:S(2)}) collective-permute-start(f32[16,128,128]{2,1,0:T(8,128)S(1)} %get-tuple-element.8), channel_id=1, source_target_pairs={{0,4},{4,0},{1,5},{5,1},{2,6},{6,2},{3,7},{7,3},{8,12},{12,8},{9,1... | collective-permute-start | bytes 3145736 | tf_op jit(solution)/shard_map/ppermute | solution.py:268
  13.9 1.0 keep_image.1
  15.0 1.2 %collective-permute-done = f32[16,128,128]{2,1,0:T(8,128)S(1)} collective-permute-done((f32[16,128,128]{2,1,0:T(8,128)S(1)}, f32[16,128,128]{2,1,0:T(8,128)S(1)}, u32[]{:S(2)}, u32[]{:S(2)}) %collective-permute-start) | collective-permute-done | bytes 1048608 | tf_op jit(solution)/shard_map/ppermute | solution.py:268
  16.2 0.2 add.34
  16.3 0.0 copy-start
  16.4 20.3 %all_to_all.15 = f32[32,64,128]{2,1,0:T(8,128)S(1)} all-to-all(f32[32,64,128]{2,1,0:T(8,128)S(1)} %bitcast.7), channel_id=1, replica_groups=mesh['y'=4,'z_pair'=8,'z_in_pair'=2,'core'=2,'x'=4] {'x','y','z_in_pair'}, dimensions={0} | all-to-all | bytes 2097152 | tf_op jit(solution)/shard_map/all_to_all | solution.py:254
  36.7 0.1 reduce_sum.18
  36.8 30.8 %all_to_all.16 = f32[8,64,128]{2,1,0:T(8,128)S(1)} all-to-all(f32[8,64,128]{2,1,0:T(8,128)S(1)} %broadcast_in_dim.4), channel_id=1, replica_groups=mesh['y'=4,'z_pair'=8,'z_in_pair'=2,'core'=2,'x'=4] {'z_pair'}, dimensions={0} | all-to-all | bytes 524288 | tf_op jit(solution)/shard_map/all_to_all | solution.py:254
  67.7 0.1 broadcast_in_dim.5
  67.8 20.2 %all_to_all.17 = f32[32,64,128]{2,1,0:T(8,128)S(1)} all-to-all(f32[32,64,128]{2,1,0:T(8,128)S(1)} %broadcast_in_dim.5), channel_id=1, replica_groups=mesh['y'=4,'z_pair'=8,'z_in_pair'=2,'core'=2,'x'=4] {'x','y','z_in_pair'}, dimensions={0} | all-to-all | bytes 2097152 | tf_op jit(solution)/shard_map/all_to_all | solution.py:254
  88.0 4.8 %collective-permute-start.1 = (f32[16,128,128]{2,1,0:T(8,128)S(1)}, f32[16,128,128]{2,1,0:T(8,128)S(1)}, u32[]{:S(2)}, u32[]{:S(2)}) collective-permute-start(f32[16,128,128]{2,1,0:T(8,128)S(1)} %bitcast.5), channel_id=1, source_target_pairs={{0,4},{4,0},{1,5},{5,1},{2,6},{6,2},{3,7},{7,3},{8,12},{12,8},{9,1... | collective-permute-start | bytes 3145736 | tf_op jit(solution)/shard_map/ppermute | solution.py:268
  92.9 0.1 pad_add_fusion.place_ref
  93.0 1.9 %collective-permute-done.1.other_ref = f32[16,128,128]{2,1,0:T(8,128)S(1)} collective-permute-done((f32[16,128,128]{2,1,0:T(8,128)S(1)}, f32[16,128,128]{2,1,0:T(8,128)S(1)}, u32[]{:S(2)}, u32[]{:S(2)}) %collective-permute-start.1) | collective-permute-done | bytes 1048608 | tf_op jit(solution)/shard_map/ppermute | solution.py:268
  94.9 0.0 copy-done
  94.9 12.6 %finish.1 = (f32[224,128]{1,0:T(8,128)}, f32[8,128]{1,0:T(8,128)}, f32[128,128]{1,0:T(8,128)}) custom-call(s32[3]{0:T(128)S(1)} %pad_add_fusion.place_ref, f32[16,128,128]{2,1,0:T(8,128)S(1)} %bitcast.6, f32[16,128,128]{2,1,0:T(8,128)S(1)} %collective-permute-done.1.other_ref, f32[224,128]{1,0:T(8,128)S(1)} %get-tuple-element.6.sketch_ref, ...), custom_call_target="tpu_custom_call" | custom-call | tf_op jit(solution)/shard_map/finish/pallas_call | solution.py:235
  (2 shorter events, 0.0 us)
Async XLA Ops:
  5.1 11.1 %collective-permute-start = (f32[16,128,128]{2,1,0:T(8,128)S(1)}, f32[16,128,128]{2,1,0:T(8,128)S(1)}, u32[]{:S(2)}, u32[]{:S(2)}) collective-permute-start(f32[16,128,128]{2,1,0:T(8,128)S(1)} %get-tuple-element.8), channel_id=1, source_target_pairs={{0,4},{4,0},{1,5},{5,1},{2,6},{6,2},{3,7},{7,3},{8,12},{12,8},{9,1... | collective-permute-start | bytes 3145736 | tf_op jit(solution)/shard_map/ppermute | solution.py:268
  16.3 78.6 %copy-start = (bf16[4096,128]{1,0:T(8,128)(2,1)S(1)}, bf16[4096,128]{1,0:T(8,128)(2,1)}, u32[]{:S(2)}) copy-start(bf16[4096,128]{1,0:T(8,128)(2,1)} %test_ref.1) | copy-start | bytes 3145732
  88.0 6.9 %collective-permute-start.1 = (f32[16,128,128]{2,1,0:T(8,128)S(1)}, f32[16,128,128]{2,1,0:T(8,128)S(1)}, u32[]{:S(2)}, u32[]{:S(2)}) collective-permute-start(f32[16,128,128]{2,1,0:T(8,128)S(1)} %bitcast.5), channel_id=1, source_target_pairs={{0,4},{4,0},{1,5},{5,1},{2,6},{6,2},{3,7},{7,3},{8,12},{12,8},{9,1... | collective-permute-start | bytes 3145736 | tf_op jit(solution)/shard_map/ppermute | solution.py:268

commit v5 on v4

--- a/solution.py
+++ b/solution.py
@@ -12,6 +12,7 @@
 CHUNKS = 4
 STEP = 512
 PANEL = 32
+SPREAD = 2.0
 LANES = 128
 F32, BF16 = jnp.float32, jnp.bfloat16
 VMEM_LIMIT = 24 * 1024 * 1024
@@ -158,10 +159,11 @@
                     factor = jnp.where(sublane > i, factor, 0.0)
                 a[q] = a[q] - factor * row_a
                 b[q] = b[q] - factor * row_b
+            yield
         column = {q: column[q][8:] for q in tiles[g + 1 :]}
 
 
-def factorize(gram):
+def factor_steps(gram, result):
     size = gram.shape[0]
     tiles = lambda value: [value[8 * t : 8 * t + 8] for t in range(PANEL // 8)]
     row = lax.broadcasted_iota(jnp.int32, (size, size), 0)
@@ -170,7 +172,7 @@
     uppers, inverses = [], []
     for start in range(0, size, PANEL):
         a, b = tiles(gram), tiles(other)
-        eliminate(a, b, start)
+        yield from eliminate(a, b, start)
         a, b = jnp.concatenate(a, axis=0), jnp.concatenate(b, axis=0)
         here = row[start : start + PANEL]
         lanes = column[start : start + PANEL]
@@ -178,56 +180,80 @@
         upper, inverse = jnp.where(lanes >= here, a * scale, 0.0), b * scale
         uppers.append(upper)
         inverses.append(inverse)
+        yield
         if start + PANEL < size:
             below = split(upper.T[start + PANEL :])
             change = dot_split(below, split(jnp.concatenate([upper, inverse], axis=1)))
             gram, other = gram[PANEL:] - change[:, :size], other[PANEL:] - change[:, size:]
-    return jnp.concatenate(uppers, axis=0), jnp.concatenate(inverses, axis=0)
+        yield
+    result += [jnp.concatenate(uppers, axis=0), jnp.concatenate(inverses, axis=0)]
+
+
+def factorize(*grams):
+    results = [[] for _ in grams]
+    for _ in zip(*(factor_steps(gram, result) for gram, result in zip(grams, results, strict=True)), strict=True):
+        pass
+    return results
+
+
+def self_products(terms):
+    cross = dot(terms[1], terms[0], 1) + dot(terms[2], terms[0], 1)
+    return dot(terms[0], terms[0], 1) + (cross + cross.T + dot(terms[1], terms[1], 1))
 
 
 def finish_kernel(
     total_rows, place_ref, mine_ref, other_ref, sketch_ref, test_ref,
-    basis_ref, right_ref, factor_ref, loadings, turned,
+    basis_ref, right_ref, factor_ref, loadings, inverse_first, turned,
 ):
     blocks = mine_ref.shape[0]
-    group = 16
+    width = 2 * blocks * LANES
     core = place_ref[0]
-    halves = ((mine_ref, core), (other_ref, 1 - core))
-
-    def wide(ref, first):
-        return jnp.concatenate([ref[first + b] for b in range(group)], axis=1)
-
-    partial = []
-    for ref, half in halves:
-        total = jnp.zeros((LANES, LANES), F32)
-        for first in range(0, blocks, group):
-            terms = split(wide(ref, first))
-            offset = pl.multiple_of((half * blocks + first) * LANES, group * LANES)
-            test = test_ref[pl.ds(offset, group * LANES), :]
-            total += dot(terms[0], test) + (dot(terms[1], test) + dot(terms[2], test))
-        partial.append(total)
-    gram = (partial[0] + partial[1]) * (0.5 / total_rows)
-    _, inverse = factorize(gram + gram.T)
+
+    def wide(ref):
+        return jnp.concatenate([ref[b] for b in range(blocks)], axis=1)
+
+    def write_right(inverse, block):
+        turned[...] = dot_split(split(inverse), split(block)).T
+        right_ref[...] = turned[pl.ds(pl.multiple_of(place_ref[2], 8), right_ref.shape[0]), :]
+
+    sketch_parts, image_parts = [], []
+    for ref, half in ((mine_ref, core), (other_ref, 1 - core)):
+        terms = split(wide(ref))
+        test = test_ref[pl.ds(pl.multiple_of(half * blocks * LANES, blocks * LANES), blocks * LANES), :]
+        sketch_parts.append(dot(terms[0], test) + (dot(terms[1], test) + dot(terms[2], test)))
+        image_parts.append(self_products(terms))
+    gram = (sketch_parts[0] + sketch_parts[1]) * (0.5 / total_rows)
+    image_gram = (image_parts[0] + image_parts[1]) * (1.0 / width)
+    (_, inverse), (upper_image, inverse_image) = factorize(gram + gram.T, image_gram)
     left = split(inverse)
-
-    partial = []
-    for h, (ref, _) in enumerate(halves):
-        total, cross, small = (jnp.zeros((LANES, LANES), F32) for _ in range(3))
-        for first in range(0, blocks, group):
-            values = dot_split(left, split(wide(ref, first)))
-            for b in range(group):
-                loadings[h * blocks + first + b] = values[:, b * LANES : (b + 1) * LANES]
-            terms = split(values)
-            total += dot(terms[0], terms[0], 1)
-            cross += dot(terms[1], terms[0], 1) + dot(terms[2], terms[0], 1)
-            small += dot(terms[1], terms[1], 1)
-        partial.append(total + (cross + cross.T + small))
-    upper, second = factorize((partial[0] + partial[1]) / (2 * blocks * LANES))
-    factor_ref[...] = upper.T
-
+    inverse_first[...] = inverse
     basis_ref[...] = dot_split(split(sketch_ref[...]), left, 1)
-    turned[...] = dot_split(split(second), split(loadings[place_ref[1]])).T
-    right_ref[...] = turned[pl.ds(pl.multiple_of(place_ref[2], 8), right_ref.shape[0]), :]
+    factor_ref[...] = dot_split(left, split(upper_image), 1)
+    slot = lax.rem(place_ref[1], blocks)
+    write_right(inverse_image, jnp.where(place_ref[1] < blocks, mine_ref[slot], other_ref[slot]))
+
+    row = lax.broadcasted_iota(jnp.int32, (LANES, LANES), 0)
+    column = lax.broadcasted_iota(jnp.int32, (LANES, LANES), 1)
+    trace = jnp.sum(jnp.where(row == column, image_gram, 0.0))
+    spread = trace * jnp.sum(inverse_image * inverse_image)
+
+    @pl.when(jnp.logical_not(spread <= SPREAD * LANES * LANES))
+    def _():
+        left = split(inverse_first[...])
+        pair = jnp.concatenate([left[0], left[1]], axis=1)
+        parts = []
+        for h, ref in enumerate((mine_ref, other_ref)):
+            x = split(wide(ref))
+            values = dot(pair, jnp.concatenate([x[0], x[0]], axis=0)) + (
+                dot(pair, jnp.concatenate([x[1], x[1]], axis=0))
+                + dot(jnp.concatenate([left[2], left[0]], axis=1), jnp.concatenate([x[0], x[2]], axis=0))
+            )
+            for b in range(blocks):
+                loadings[h * blocks + b] = values[:, b * LANES : (b + 1) * LANES]
+            parts.append(self_products(split(values)))
+        ((upper, second),) = factorize((parts[0] + parts[1]) * (1.0 / width))
+        factor_ref[...] = upper.T
+        write_right(second, loadings[place_ref[1]])
 
 
 def finish(place, mine, other, sketch, test_matrix, total_rows, own_rows):
@@ -243,6 +269,7 @@
         out_specs=[vmem] * 3,
         scratch_shapes=[
             pltpu.VMEM((2 * mine.shape[0], LANES, LANES), F32),
+            pltpu.VMEM((LANES, LANES), F32),
             pltpu.VMEM((LANES, LANES), F32),
         ],
         compiler_params=pltpu.CompilerParams(vmem_limit_bytes=VMEM_LIMIT),

time: 108 us -> 110 us (1.019)
  Pallas kernels: 18.1 us -> 20.6 us
    pallas_call x1, Pallas kernels: 12.6 us -> 15.1 us  [finish(): pl.pallas_call(functools.partial(finish_kernel, total_rows), out_shape=[j...]
where the time goes in v5:
time: 110 us
  blocking collectives  71.4 us (65%)
  Pallas kernels  20.6 us (19%)
  starting transfers between devices  13.4 us (12%)
  waiting for transfers between devices  3.36 us (3%)
    all_to_all x3, blocking collectives, exchange(): return lax.all_to_all(values, axes, 0, 0, tiled=False)  71.4 us
    pallas_call x1, Pallas kernels, finish(): pl.pallas_call(functools.partial(finish_kernel, total_rows), out_shape=[j...  15.1 us
    ppermute x2, starting transfers between devices, swap_cores(): return lax.ppermute(values, 'core', [(0, 1), (1, 0)])  13.4 us
    pallas_call x1, Pallas kernels, local_sketch(): pl.pallas_call(sketch_kernel, out_shape=[pltpu.VMEM((rows, LANES), F32),...  4.49 us
    ppermute x2, waiting for transfers between devices, swap_cores(): return lax.ppermute(values, 'core', [(0, 1), (1, 0)])  3.36 us
  transfers between devices with their start and end apart: 2, of which 2 were waited for; matrix products, arithmetic and copies ran while one was open for 0% of the time, Pallas kernels for 1%

profile of v5, /device:TPU:1, one launch (start us, length us, event | category | flops | bytes accessed | tf_op | source)
XLA Modules:
  0.0 110.0 jit_solution(8154602661259799656)
XLA Ops:
  0.6 4.5 %local_sketch.1 = (f32[224,128]{1,0:T(8,128)S(1)}, f32[16,128,128]{2,1,0:T(8,128)S(1)}, bf16[3,224,2048]{2,1,0:T(8,128)(2,1)S(1)}) custom-call(s32[1]{0:T(128)} %bitcast.core_ref, f32[224,4096]{1,0:T(8,128)} %emb_hbm.1, bf16[4096,128]{1,0:T(8,128)(2,1)} %test_ref.1), custom_call_target="tpu_custom_call" | custom-call | flops 1409286144 | bytes 3670016 | tf_op jit(solution)/shard_map/local_sketch/pallas_call | solution.py:91
  5.1 8.8 %collective-permute-start = (f32[16,128,128]{2,1,0:T(8,128)S(1)}, f32[16,128,128]{2,1,0:T(8,128)S(1)}, u32[]{:S(2)}, u32[]{:S(2)}) collective-permute-start(f32[16,128,128]{2,1,0:T(8,128)S(1)} %get-tuple-element.8), channel_id=1, source_target_pairs={{0,4},{4,0},{1,5},{5,1},{2,6},{6,2},{3,7},{7,3},{8,12},{12,8},{9,1... | collective-permute-start | bytes 3145736 | tf_op jit(solution)/shard_map/ppermute | solution.py:295
  13.9 1.0 keep_image.1
  15.0 1.2 %collective-permute-done = f32[16,128,128]{2,1,0:T(8,128)S(1)} collective-permute-done((f32[16,128,128]{2,1,0:T(8,128)S(1)}, f32[16,128,128]{2,1,0:T(8,128)S(1)}, u32[]{:S(2)}, u32[]{:S(2)}) %collective-permute-start) | collective-permute-done | bytes 1048608 | tf_op jit(solution)/shard_map/ppermute | solution.py:295
  16.2 0.2 add.34
  16.3 0.0 copy-start
  16.4 20.3 %all_to_all.15 = f32[32,64,128]{2,1,0:T(8,128)S(1)} all-to-all(f32[32,64,128]{2,1,0:T(8,128)S(1)} %bitcast.7), channel_id=1, replica_groups=mesh['y'=4,'z_pair'=8,'z_in_pair'=2,'core'=2,'x'=4] {'x','y','z_in_pair'}, dimensions={0} | all-to-all | bytes 2097152 | tf_op jit(solution)/shard_map/all_to_all | solution.py:281
  36.7 0.1 reduce_sum.18
  36.8 30.8 %all_to_all.16 = f32[8,64,128]{2,1,0:T(8,128)S(1)} all-to-all(f32[8,64,128]{2,1,0:T(8,128)S(1)} %broadcast_in_dim.4), channel_id=1, replica_groups=mesh['y'=4,'z_pair'=8,'z_in_pair'=2,'core'=2,'x'=4] {'z_pair'}, dimensions={0} | all-to-all | bytes 524288 | tf_op jit(solution)/shard_map/all_to_all | solution.py:281
  67.7 0.1 broadcast_in_dim.5
  67.8 20.2 %all_to_all.17 = f32[32,64,128]{2,1,0:T(8,128)S(1)} all-to-all(f32[32,64,128]{2,1,0:T(8,128)S(1)} %broadcast_in_dim.5), channel_id=1, replica_groups=mesh['y'=4,'z_pair'=8,'z_in_pair'=2,'core'=2,'x'=4] {'x','y','z_in_pair'}, dimensions={0} | all-to-all | bytes 2097152 | tf_op jit(solution)/shard_map/all_to_all | solution.py:281
  88.0 4.6 %collective-permute-start.1 = (f32[16,128,128]{2,1,0:T(8,128)S(1)}, f32[16,128,128]{2,1,0:T(8,128)S(1)}, u32[]{:S(2)}, u32[]{:S(2)}) collective-permute-start(f32[16,128,128]{2,1,0:T(8,128)S(1)} %bitcast.5), channel_id=1, source_target_pairs={{0,4},{4,0},{1,5},{5,1},{2,6},{6,2},{3,7},{7,3},{8,12},{12,8},{9,1... | collective-permute-start | bytes 3145736 | tf_op jit(solution)/shard_map/ppermute | solution.py:295
  92.7 0.1 pad_add_fusion.place_ref
  92.8 2.1 %collective-permute-done.1.other_ref = f32[16,128,128]{2,1,0:T(8,128)S(1)} collective-permute-done((f32[16,128,128]{2,1,0:T(8,128)S(1)}, f32[16,128,128]{2,1,0:T(8,128)S(1)}, u32[]{:S(2)}, u32[]{:S(2)}) %collective-permute-start.1) | collective-permute-done | bytes 1048608 | tf_op jit(solution)/shard_map/ppermute | solution.py:295
  94.9 0.0 copy-done
  94.9 15.1 %finish.1 = (f32[224,128]{1,0:T(8,128)}, f32[8,128]{1,0:T(8,128)}, f32[128,128]{1,0:T(8,128)}) custom-call(s32[3]{0:T(128)S(1)} %pad_add_fusion.place_ref, f32[16,128,128]{2,1,0:T(8,128)S(1)} %bitcast.6, f32[16,128,128]{2,1,0:T(8,128)S(1)} %collective-permute-done.1.other_ref, f32[224,128]{1,0:T(8,128)S(1)} %get-tuple-element.6.sketch_ref, ...), custom_call_target="tpu_custom_call" | custom-call | tf_op jit(solution)/shard_map/finish/pallas_call | solution.py:261
  (2 shorter events, 0.0 us)
Async XLA Ops:
  5.1 11.1 %collective-permute-start = (f32[16,128,128]{2,1,0:T(8,128)S(1)}, f32[16,128,128]{2,1,0:T(8,128)S(1)}, u32[]{:S(2)}, u32[]{:S(2)}) collective-permute-start(f32[16,128,128]{2,1,0:T(8,128)S(1)} %get-tuple-element.8), channel_id=1, source_target_pairs={{0,4},{4,0},{1,5},{5,1},{2,6},{6,2},{3,7},{7,3},{8,12},{12,8},{9,1... | collective-permute-start | bytes 3145736 | tf_op jit(solution)/shard_map/ppermute | solution.py:295
  16.3 78.6 %copy-start = (bf16[4096,128]{1,0:T(8,128)(2,1)S(1)}, bf16[4096,128]{1,0:T(8,128)(2,1)}, u32[]{:S(2)}) copy-start(bf16[4096,128]{1,0:T(8,128)(2,1)} %test_ref.1) | copy-start | bytes 3145732
  88.0 6.9 %collective-permute-start.1 = (f32[16,128,128]{2,1,0:T(8,128)S(1)}, f32[16,128,128]{2,1,0:T(8,128)S(1)}, u32[]{:S(2)}, u32[]{:S(2)}) collective-permute-start(f32[16,128,128]{2,1,0:T(8,128)S(1)} %bitcast.5), channel_id=1, source_target_pairs={{0,4},{4,0},{1,5},{5,1},{2,6},{6,2},{3,7},{7,3},{8,12},{12,8},{9,1... | collective-permute-start | bytes 3145736 | tf_op jit(solution)/shard_map/ppermute | solution.py:295

commit v6 on v5

--- a/solution.py
+++ b/solution.py
@@ -10,7 +10,7 @@
 AXES = ("y", "z_pair", "z_in_pair", "core", "x")
 NEAR = ("x", "y", "z_in_pair")
 CHUNKS = 4
-STEP = 512
+STEP = 2048
 PANEL = 32
 SPREAD = 2.0
 LANES = 128
@@ -141,26 +141,31 @@
 
 def eliminate(a, b, first_lane):
     sublane = lax.broadcasted_iota(jnp.int32, (8, LANES), 0)
-    tiles = range(len(a))
-    column = {q: [over_lanes(a[q], first_lane + k) for k in range(8)] for q in tiles}
-    for g in tiles:
-        if g + 1 < len(a):
-            for q in tiles[g:]:
-                column[q] = column[q] + [over_lanes(a[q], first_lane + 8 * g + k) for k in range(8, 16)]
+    spread = lambda tile, first: [over_lanes(tile, first + k) for k in range(8)]
+    last = len(a) - 1
+    ahead = spread(a[0], first_lane)
+    for g in range(last + 1):
+        first = first_lane + 8 * g
+        column = {q: spread(a[q], first) for q in range(g + 1, last + 1)}
+        column[g] = ahead
+        if g < last:
+            column[g] = column[g] + spread(a[g], first + 8)
+            column[g + 1] = column[g + 1] + spread(a[g + 1], first + 8)
         for i in range(8):
             pivots = [over_sublanes(values, i) for values in column[g]]
             inverse = 1.0 / pivots[i]
             row_a, row_b = over_sublanes(a[g], i), over_sublanes(b[g], i)
-            for q in tiles[g:]:
+            for q in range(g, last + 1):
                 factor = column[q][i] * inverse
-                for k in range(i + 1, len(pivots)):
+                for k in range(i + 1, len(column[q])):
                     column[q][k] = column[q][k] - factor * pivots[k]
                 if q == g:
                     factor = jnp.where(sublane > i, factor, 0.0)
                 a[q] = a[q] - factor * row_a
                 b[q] = b[q] - factor * row_b
             yield
-        column = {q: column[q][8:] for q in tiles[g + 1 :]}
+        if g < last:
+            ahead = column[g + 1][8:]
 
 
 def factor_steps(gram, result):
@@ -201,36 +206,50 @@
     return dot(terms[0], terms[0], 1) + (cross + cross.T + dot(terms[1], terms[1], 1))
 
 
+def grams_kernel(half_ref, ref, test_ref, grams_ref):
+    columns = ref.shape[0] * LANES
+    terms = split(jnp.concatenate([ref[b] for b in range(ref.shape[0])], axis=1))
+    test = test_ref[pl.ds(pl.multiple_of(half_ref[0] * columns, columns), columns), :]
+    grams_ref[0] = dot(terms[0], test) + (dot(terms[1], test) + dot(terms[2], test))
+    grams_ref[1] = self_products(terms)
+
+
+def half_grams(half, image, test_matrix):
+    vmem = pl.BlockSpec(memory_space=pltpu.VMEM)
+    return pl.pallas_call(
+        grams_kernel,
+        out_shape=pltpu.VMEM((2, LANES, LANES), F32),
+        in_specs=[pl.BlockSpec(memory_space=pltpu.SMEM), vmem, vmem],
+        out_specs=vmem,
+        compiler_params=pltpu.CompilerParams(vmem_limit_bytes=VMEM_LIMIT),
+        cost_estimate=pl.CostEstimate(flops=14 * LANES * image.size, bytes_accessed=4 * image.size, transcendentals=0),
+        name="half_grams",
+    )(half.reshape(1), image, test_matrix)
+
+
 def finish_kernel(
-    total_rows, place_ref, mine_ref, other_ref, sketch_ref, test_ref,
+    total_rows, place_ref, mine_grams, other_grams, mine_ref, other_ref, sketch_ref,
     basis_ref, right_ref, factor_ref, loadings, inverse_first, turned,
 ):
     blocks = mine_ref.shape[0]
     width = 2 * blocks * LANES
-    core = place_ref[0]
-
-    def wide(ref):
-        return jnp.concatenate([ref[b] for b in range(blocks)], axis=1)
+    core, own_block = place_ref[0], place_ref[1]
+
+    def image_block(half, b):
+        return jnp.where(core == half, mine_ref[b], other_ref[b])
 
     def write_right(inverse, block):
         turned[...] = dot_split(split(inverse), split(block)).T
         right_ref[...] = turned[pl.ds(pl.multiple_of(place_ref[2], 8), right_ref.shape[0]), :]
 
-    sketch_parts, image_parts = [], []
-    for ref, half in ((mine_ref, core), (other_ref, 1 - core)):
-        terms = split(wide(ref))
-        test = test_ref[pl.ds(pl.multiple_of(half * blocks * LANES, blocks * LANES), blocks * LANES), :]
-        sketch_parts.append(dot(terms[0], test) + (dot(terms[1], test) + dot(terms[2], test)))
-        image_parts.append(self_products(terms))
-    gram = (sketch_parts[0] + sketch_parts[1]) * (0.5 / total_rows)
-    image_gram = (image_parts[0] + image_parts[1]) * (1.0 / width)
+    gram = (mine_grams[0] + other_grams[0]) * (0.5 / total_rows)
+    image_gram = (mine_grams[1] + other_grams[1]) * (1.0 / width)
     (_, inverse), (upper_image, inverse_image) = factorize(gram + gram.T, image_gram)
     left = split(inverse)
     inverse_first[...] = inverse
     basis_ref[...] = dot_split(split(sketch_ref[...]), left, 1)
     factor_ref[...] = dot_split(left, split(upper_image), 1)
-    slot = lax.rem(place_ref[1], blocks)
-    write_right(inverse_image, jnp.where(place_ref[1] < blocks, mine_ref[slot], other_ref[slot]))
+    write_right(inverse_image, image_block(own_block // blocks, lax.rem(own_block, blocks)))
 
     row = lax.broadcasted_iota(jnp.int32, (LANES, LANES), 0)
     column = lax.broadcasted_iota(jnp.int32, (LANES, LANES), 1)
@@ -242,21 +261,21 @@
         left = split(inverse_first[...])
         pair = jnp.concatenate([left[0], left[1]], axis=1)
         parts = []
-        for h, ref in enumerate((mine_ref, other_ref)):
-            x = split(wide(ref))
+        for half in range(2):
+            x = split(jnp.concatenate([image_block(half, b) for b in range(blocks)], axis=1))
             values = dot(pair, jnp.concatenate([x[0], x[0]], axis=0)) + (
                 dot(pair, jnp.concatenate([x[1], x[1]], axis=0))
                 + dot(jnp.concatenate([left[2], left[0]], axis=1), jnp.concatenate([x[0], x[2]], axis=0))
             )
             for b in range(blocks):
-                loadings[h * blocks + b] = values[:, b * LANES : (b + 1) * LANES]
+                loadings[half * blocks + b] = values[:, b * LANES : (b + 1) * LANES]
             parts.append(self_products(split(values)))
         ((upper, second),) = factorize((parts[0] + parts[1]) * (1.0 / width))
         factor_ref[...] = upper.T
-        write_right(second, loadings[place_ref[1]])
-
-
-def finish(place, mine, other, sketch, test_matrix, total_rows, own_rows):
+        write_right(second, loadings[own_block])
+
+
+def finish(place, mine_grams, other_grams, mine, other, sketch, total_rows, own_rows):
     vmem = pl.BlockSpec(memory_space=pltpu.VMEM)
     return pl.pallas_call(
         functools.partial(finish_kernel, total_rows),
@@ -265,7 +284,7 @@
             jax.ShapeDtypeStruct((own_rows, LANES), F32),
             jax.ShapeDtypeStruct((LANES, LANES), F32),
         ],
-        in_specs=[pl.BlockSpec(memory_space=pltpu.SMEM)] + [vmem] * 4,
+        in_specs=[pl.BlockSpec(memory_space=pltpu.SMEM)] + [vmem] * 5,
         out_specs=[vmem] * 3,
         scratch_shapes=[
             pltpu.VMEM((2 * mine.shape[0], LANES, LANES), F32),
@@ -274,7 +293,7 @@
         ],
         compiler_params=pltpu.CompilerParams(vmem_limit_bytes=VMEM_LIMIT),
         name="finish",
-    )(place, mine, other, sketch, test_matrix)
+    )(place, mine_grams, other_grams, mine, other, sketch)
 
 
 def exchange(values, axes):
@@ -307,12 +326,11 @@
     piece = jnp.sum(copies(piece, "z_pair"), axis=0)
     mine = copies(piece, NEAR).reshape(image.shape)
     other = swap_cores(mine)
+    mine_grams = half_grams(core, mine, test_matrix)
+    other_grams = half_grams(1 - core, other, test_matrix)
     first = lax.axis_index(AXES) * own_rows
-    half_blocks = mine.shape[0]
-    own_block = first // LANES
-    slot = jnp.where(own_block // half_blocks == core, 0, half_blocks) + own_block % half_blocks
-    place = jnp.stack([core, slot, first % LANES])
-    basis, right_basis, factor = finish(place, mine, other, sketch, test_matrix, rows * devices_all, own_rows)
+    place = jnp.stack([core, first // LANES, first % LANES])
+    basis, right_basis, factor = finish(place, mine_grams, other_grams, mine, other, sketch, rows * devices_all, own_rows)
     return (basis, right_basis, factor)
 
 

time: 110 us -> 109 us (level)
  waiting for transfers between devices: 3.36 us -> 2.15 us
    pallas_call x0 -> x2, Pallas kernels: none -> 2.45 us  [half_grams(): pl.pallas_call(grams_kernel, out_shape=pltpu.VMEM((2, LANES, LANES), F32)...]
    pallas_call x1, Pallas kernels: 15.1 us -> 12.8 us  [finish(): pl.pallas_call(functools.partial(finish_kernel, total_rows), out_shape=[j...]
    ppermute x2, waiting for transfers between devices: 3.36 us -> 2.15 us  [swap_cores(): return lax.ppermute(values, 'core', [(0, 1), (1, 0)])]
  transfers between devices with their start and end apart: 2 -> 2, of which waited for: 2 -> 2; matrix products, arithmetic and copies ran while one was open for 0% -> 0% of each run, Pallas kernels for 1% -> 2%
where the time goes in v6:
time: 109 us
  blocking collectives  71.4 us (66%)
  Pallas kernels  20.8 us (19%)
  starting transfers between devices  13.4 us (12%)
  waiting for transfers between devices  2.15 us (2%)
    all_to_all x3, blocking collectives, exchange(): return lax.all_to_all(values, axes, 0, 0, tiled=False)  71.4 us
    ppermute x2, starting transfers between devices, swap_cores(): return lax.ppermute(values, 'core', [(0, 1), (1, 0)])  13.4 us
    pallas_call x1, Pallas kernels, finish(): pl.pallas_call(functools.partial(finish_kernel, total_rows), out_shape=[j...  12.8 us
    pallas_call x1, Pallas kernels, local_sketch(): pl.pallas_call(sketch_kernel, out_shape=[pltpu.VMEM((rows, LANES), F32),...  4.48 us
    pallas_call x2, Pallas kernels, half_grams(): pl.pallas_call(grams_kernel, out_shape=pltpu.VMEM((2, LANES, LANES), F32)...  2.45 us
  transfers between devices with their start and end apart: 2, of which 2 were waited for; matrix products, arithmetic and copies ran while one was open for 0% of the time, Pallas kernels for 2%

profile of v6, /device:TPU:1, one launch (start us, length us, event | category | flops | bytes accessed | tf_op | source)
XLA Modules:
  0.0 109.0 jit_solution(13654485397940211973)
XLA Ops:
  0.6 4.5 %local_sketch.1 = (f32[224,128]{1,0:T(8,128)S(1)}, f32[16,128,128]{2,1,0:T(8,128)S(1)}, bf16[3,224,2048]{2,1,0:T(8,128)(2,1)S(1)}) custom-call(s32[1]{0:T(128)} %bitcast.core_ref.half_ref, f32[224,4096]{1,0:T(8,128)} %emb_hbm.1, bf16[4096,128]{1,0:T(8,128)(2,1)} %test_ref.3), custom_call_target="tpu_custom_call" | custom-call | flops 1409286144 | bytes 3670016 | tf_op jit(solution)/shard_map/local_sketch/pallas_call | solution.py:91
  5.1 8.8 %collective-permute-start = (f32[16,128,128]{2,1,0:T(8,128)S(1)}, f32[16,128,128]{2,1,0:T(8,128)S(1)}, u32[]{:S(2)}, u32[]{:S(2)}) collective-permute-start(f32[16,128,128]{2,1,0:T(8,128)S(1)} %get-tuple-element.8), channel_id=1, source_target_pairs={{0,4},{4,0},{1,5},{5,1},{2,6},{6,2},{3,7},{7,3},{8,12},{12,8},{9,1... | collective-permute-start | bytes 3145736 | tf_op jit(solution)/shard_map/ppermute | solution.py:314
  13.9 1.0 keep_image.1
  15.0 1.2 %collective-permute-done = f32[16,128,128]{2,1,0:T(8,128)S(1)} collective-permute-done((f32[16,128,128]{2,1,0:T(8,128)S(1)}, f32[16,128,128]{2,1,0:T(8,128)S(1)}, u32[]{:S(2)}, u32[]{:S(2)}) %collective-permute-start) | collective-permute-done | bytes 1048608 | tf_op jit(solution)/shard_map/ppermute | solution.py:314
  16.2 0.2 add.25
  16.3 0.0 copy-start
  16.4 20.3 %all_to_all.15 = f32[32,64,128]{2,1,0:T(8,128)S(1)} all-to-all(f32[32,64,128]{2,1,0:T(8,128)S(1)} %bitcast.9), channel_id=1, replica_groups=mesh['y'=4,'z_pair'=8,'z_in_pair'=2,'core'=2,'x'=4] {'x','y','z_in_pair'}, dimensions={0} | all-to-all | bytes 2097152 | tf_op jit(solution)/shard_map/all_to_all | solution.py:300
  36.7 0.1 reduce_sum.18
  36.8 30.8 %all_to_all.16 = f32[8,64,128]{2,1,0:T(8,128)S(1)} all-to-all(f32[8,64,128]{2,1,0:T(8,128)S(1)} %broadcast_in_dim.4), channel_id=1, replica_groups=mesh['y'=4,'z_pair'=8,'z_in_pair'=2,'core'=2,'x'=4] {'z_pair'}, dimensions={0} | all-to-all | bytes 524288 | tf_op jit(solution)/shard_map/all_to_all | solution.py:300
  67.6 0.1 broadcast_in_dim.5
  67.8 20.2 %all_to_all.17 = f32[32,64,128]{2,1,0:T(8,128)S(1)} all-to-all(f32[32,64,128]{2,1,0:T(8,128)S(1)} %broadcast_in_dim.5), channel_id=1, replica_groups=mesh['y'=4,'z_pair'=8,'z_in_pair'=2,'core'=2,'x'=4] {'x','y','z_in_pair'}, dimensions={0} | all-to-all | bytes 2097152 | tf_op jit(solution)/shard_map/all_to_all | solution.py:300
  88.0 4.6 %collective-permute-start.1 = (f32[16,128,128]{2,1,0:T(8,128)S(1)}, f32[16,128,128]{2,1,0:T(8,128)S(1)}, u32[]{:S(2)}, u32[]{:S(2)}) collective-permute-start(f32[16,128,128]{2,1,0:T(8,128)S(1)} %bitcast.6), channel_id=1, source_target_pairs={{0,4},{4,0},{1,5},{5,1},{2,6},{6,2},{3,7},{7,3},{8,12},{12,8},{9,1... | collective-permute-start | bytes 3145736 | tf_op jit(solution)/shard_map/ppermute | solution.py:314
  92.7 0.1 pad_add_fusion.place_ref
  92.8 0.0 copy-done
  92.8 1.2 %half_grams.2.mine_grams = f32[2,128,128]{2,1,0:T(8,128)S(1)} custom-call(s32[1]{0:T(128)} %bitcast.core_ref.half_ref, f32[16,128,128]{2,1,0:T(8,128)S(1)} %bitcast.7, bf16[4096,128]{1,0:T(8,128)(2,1)S(1)} %copy-done), custom_call_target="tpu_custom_call" | custom-call | flops 469762048 | bytes 1048576 | tf_op jit(solution)/shard_map/half_grams/pallas_call | solution.py:219
  94.0 0.9 collective-permute-done.1.ref.other_ref
  94.9 1.2 %half_grams.3.other_grams = f32[2,128,128]{2,1,0:T(8,128)S(1)} custom-call(s32[1]{0:T(128)} %bitcast.5.half_ref, f32[16,128,128]{2,1,0:T(8,128)S(1)} %collective-permute-done.1.ref.other_ref, bf16[4096,128]{1,0:T(8,128)(2,1)S(1)} %copy-done), custom_call_target="tpu_custom_call" | custom-call | flops 469762048 | bytes 1048576 | tf_op jit(solution)/shard_map/half_grams/pallas_call | solution.py:219
  96.2 12.8 %finish.1 = (f32[224,128]{1,0:T(8,128)}, f32[8,128]{1,0:T(8,128)}, f32[128,128]{1,0:T(8,128)}) custom-call(s32[3]{0:T(128)S(1)} %pad_add_fusion.place_ref, f32[2,128,128]{2,1,0:T(8,128)S(1)} %half_grams.2.mine_grams, f32[2,128,128]{2,1,0:T(8,128)S(1)} %half_grams.3.other_grams, f32[16,128,128]{2,1,0:T(8,128)S(1)} %bitcast.8, ...), custom_call_target="tpu_custom_call" | custom-call | tf_op jit(solution)/shard_map/finish/pallas_call | solution.py:280
  (2 shorter events, 0.0 us)
Async XLA Ops:
  5.1 11.1 %collective-permute-start = (f32[16,128,128]{2,1,0:T(8,128)S(1)}, f32[16,128,128]{2,1,0:T(8,128)S(1)}, u32[]{:S(2)}, u32[]{:S(2)}) collective-permute-start(f32[16,128,128]{2,1,0:T(8,128)S(1)} %get-tuple-element.8), channel_id=1, source_target_pairs={{0,4},{4,0},{1,5},{5,1},{2,6},{6,2},{3,7},{7,3},{8,12},{12,8},{9,1... | collective-permute-start | bytes 3145736 | tf_op jit(solution)/shard_map/ppermute | solution.py:314
  16.3 76.4 %copy-start = (bf16[4096,128]{1,0:T(8,128)(2,1)S(1)}, bf16[4096,128]{1,0:T(8,128)(2,1)}, u32[]{:S(2)}) copy-start(bf16[4096,128]{1,0:T(8,128)(2,1)} %test_ref.3) | copy-start | bytes 3145732
  88.0 6.9 %collective-permute-start.1 = (f32[16,128,128]{2,1,0:T(8,128)S(1)}, f32[16,128,128]{2,1,0:T(8,128)S(1)}, u32[]{:S(2)}, u32[]{:S(2)}) collective-permute-start(f32[16,128,128]{2,1,0:T(8,128)S(1)} %bitcast.6), channel_id=1, source_target_pairs={{0,4},{4,0},{1,5},{5,1},{2,6},{6,2},{3,7},{7,3},{8,12},{12,8},{9,1... | collective-permute-start | bytes 3145736 | tf_op jit(solution)/shard_map/ppermute | solution.py:314

commit v7 on v6

--- a/solution.py
+++ b/solution.py
@@ -8,7 +8,7 @@
 from jax.sharding import Mesh, PartitionSpec as P
 
 AXES = ("y", "z_pair", "z_in_pair", "core", "x")
-NEAR = ("x", "y", "z_in_pair")
+NEAR = ("z_in_pair", "x", "y")
 CHUNKS = 4
 STEP = 2048
 PANEL = 32

time: 109 us -> 108 us (level)
  blocking collectives: 71.4 us -> 68.9 us
  starting transfers between devices: 13.4 us -> 15.1 us
    all_to_all x3, blocking collectives: 71.4 us -> 68.9 us  [exchange(): return lax.all_to_all(values, axes, 0, 0, tiled=False)]
    ppermute x2, starting transfers between devices: 13.4 us -> 15.1 us  [swap_cores(): return lax.ppermute(values, 'core', [(0, 1), (1, 0)])]
where the time goes in v7:
time: 108 us
  blocking collectives  68.9 us (64%)
  Pallas kernels  20.8 us (19%)
  starting transfers between devices  15.1 us (14%)
  waiting for transfers between devices  2.15 us (2%)
    all_to_all x3, blocking collectives, exchange(): return lax.all_to_all(values, axes, 0, 0, tiled=False)  68.9 us
    ppermute x2, starting transfers between devices, swap_cores(): return lax.ppermute(values, 'core', [(0, 1), (1, 0)])  15.1 us
    pallas_call x1, Pallas kernels, finish(): pl.pallas_call(functools.partial(finish_kernel, total_rows), out_shape=[j...  12.8 us
    pallas_call x1, Pallas kernels, local_sketch(): pl.pallas_call(sketch_kernel, out_shape=[pltpu.VMEM((rows, LANES), F32),...  4.48 us
    pallas_call x2, Pallas kernels, half_grams(): pl.pallas_call(grams_kernel, out_shape=pltpu.VMEM((2, LANES, LANES), F32)...  2.45 us
  transfers between devices with their start and end apart: 2, of which 2 were waited for; matrix products, arithmetic and copies ran while one was open for 0% of the time, Pallas kernels for 2%

profile of v7, /device:TPU:1, one launch (start us, length us, event | category | flops | bytes accessed | tf_op | source)
XLA Modules:
  0.0 108.1 jit_solution(14200189230986966362)
XLA Ops:
  0.6 4.5 %local_sketch.1 = (f32[224,128]{1,0:T(8,128)S(1)}, f32[16,128,128]{2,1,0:T(8,128)S(1)}, bf16[3,224,2048]{2,1,0:T(8,128)(2,1)S(1)}) custom-call(s32[1]{0:T(128)} %bitcast.core_ref.half_ref, f32[224,4096]{1,0:T(8,128)} %emb_hbm.1, bf16[4096,128]{1,0:T(8,128)(2,1)} %test_ref.3), custom_call_target="tpu_custom_call" | custom-call | flops 1409286144 | bytes 3670016 | tf_op jit(solution)/shard_map/local_sketch/pallas_call | solution.py:91
  5.1 8.8 %collective-permute-start = (f32[16,128,128]{2,1,0:T(8,128)S(1)}, f32[16,128,128]{2,1,0:T(8,128)S(1)}, u32[]{:S(2)}, u32[]{:S(2)}) collective-permute-start(f32[16,128,128]{2,1,0:T(8,128)S(1)} %get-tuple-element.8), channel_id=1, source_target_pairs={{0,4},{4,0},{1,5},{5,1},{2,6},{6,2},{3,7},{7,3},{8,12},{12,8},{9,1... | collective-permute-start | bytes 3145736 | tf_op jit(solution)/shard_map/ppermute | solution.py:314
  13.9 1.0 keep_image.1
  15.0 1.2 %collective-permute-done = f32[16,128,128]{2,1,0:T(8,128)S(1)} collective-permute-done((f32[16,128,128]{2,1,0:T(8,128)S(1)}, f32[16,128,128]{2,1,0:T(8,128)S(1)}, u32[]{:S(2)}, u32[]{:S(2)}) %collective-permute-start) | collective-permute-done | bytes 1048608 | tf_op jit(solution)/shard_map/ppermute | solution.py:314
  16.2 0.2 add.25
  16.3 0.0 copy-start
  16.4 18.4 %all_to_all.15 = f32[32,64,128]{2,1,0:T(8,128)S(1)} all-to-all(f32[32,64,128]{2,1,0:T(8,128)S(1)} %bitcast.9), channel_id=1, replica_groups=mesh['y'=4,'z_pair'=8,'z_in_pair'=2,'core'=2,'x'=4] {'z_in_pair','x','y'}, dimensions={0} | all-to-all | bytes 2097152 | tf_op jit(solution)/shard_map/all_to_all | solution.py:300
  34.8 0.1 reduce_sum.18
  34.9 30.2 %all_to_all.16 = f32[8,64,128]{2,1,0:T(8,128)S(1)} all-to-all(f32[8,64,128]{2,1,0:T(8,128)S(1)} %broadcast_in_dim.4), channel_id=1, replica_groups=mesh['y'=4,'z_pair'=8,'z_in_pair'=2,'core'=2,'x'=4] {'z_pair'}, dimensions={0} | all-to-all | bytes 524288 | tf_op jit(solution)/shard_map/all_to_all | solution.py:300
  65.1 0.1 broadcast_in_dim.5
  65.2 20.3 %all_to_all.17 = f32[32,64,128]{2,1,0:T(8,128)S(1)} all-to-all(f32[32,64,128]{2,1,0:T(8,128)S(1)} %broadcast_in_dim.5), channel_id=1, replica_groups=mesh['y'=4,'z_pair'=8,'z_in_pair'=2,'core'=2,'x'=4] {'z_in_pair','x','y'}, dimensions={0} | all-to-all | bytes 2097152 | tf_op jit(solution)/shard_map/all_to_all | solution.py:300
  85.5 6.3 %collective-permute-start.1 = (f32[16,128,128]{2,1,0:T(8,128)S(1)}, f32[16,128,128]{2,1,0:T(8,128)S(1)}, u32[]{:S(2)}, u32[]{:S(2)}) collective-permute-start(f32[16,128,128]{2,1,0:T(8,128)S(1)} %bitcast.6), channel_id=1, source_target_pairs={{0,4},{4,0},{1,5},{5,1},{2,6},{6,2},{3,7},{7,3},{8,12},{12,8},{9,1... | collective-permute-start | bytes 3145736 | tf_op jit(solution)/shard_map/ppermute | solution.py:314
  91.8 0.1 pad_add_fusion.place_ref
  91.9 0.0 copy-done
  91.9 1.2 %half_grams.2.mine_grams = f32[2,128,128]{2,1,0:T(8,128)S(1)} custom-call(s32[1]{0:T(128)} %bitcast.core_ref.half_ref, f32[16,128,128]{2,1,0:T(8,128)S(1)} %bitcast.7, bf16[4096,128]{1,0:T(8,128)(2,1)S(1)} %copy-done), custom_call_target="tpu_custom_call" | custom-call | flops 469762048 | bytes 1048576 | tf_op jit(solution)/shard_map/half_grams/pallas_call | solution.py:219
  93.1 0.9 collective-permute-done.1.ref.other_ref
  94.0 1.2 %half_grams.3.other_grams = f32[2,128,128]{2,1,0:T(8,128)S(1)} custom-call(s32[1]{0:T(128)} %bitcast.5.half_ref, f32[16,128,128]{2,1,0:T(8,128)S(1)} %collective-permute-done.1.ref.other_ref, bf16[4096,128]{1,0:T(8,128)(2,1)S(1)} %copy-done), custom_call_target="tpu_custom_call" | custom-call | flops 469762048 | bytes 1048576 | tf_op jit(solution)/shard_map/half_grams/pallas_call | solution.py:219
  95.3 12.8 %finish.1 = (f32[224,128]{1,0:T(8,128)}, f32[8,128]{1,0:T(8,128)}, f32[128,128]{1,0:T(8,128)}) custom-call(s32[3]{0:T(128)S(1)} %pad_add_fusion.place_ref, f32[2,128,128]{2,1,0:T(8,128)S(1)} %half_grams.2.mine_grams, f32[2,128,128]{2,1,0:T(8,128)S(1)} %half_grams.3.other_grams, f32[16,128,128]{2,1,0:T(8,128)S(1)} %bitcast.8, ...), custom_call_target="tpu_custom_call" | custom-call | tf_op jit(solution)/shard_map/finish/pallas_call | solution.py:280
  (2 shorter events, 0.0 us)
Async XLA Ops:
  5.1 11.1 %collective-permute-start = (f32[16,128,128]{2,1,0:T(8,128)S(1)}, f32[16,128,128]{2,1,0:T(8,128)S(1)}, u32[]{:S(2)}, u32[]{:S(2)}) collective-permute-start(f32[16,128,128]{2,1,0:T(8,128)S(1)} %get-tuple-element.8), channel_id=1, source_target_pairs={{0,4},{4,0},{1,5},{5,1},{2,6},{6,2},{3,7},{7,3},{8,12},{12,8},{9,1... | collective-permute-start | bytes 3145736 | tf_op jit(solution)/shard_map/ppermute | solution.py:314
  16.3 75.5 %copy-start = (bf16[4096,128]{1,0:T(8,128)(2,1)S(1)}, bf16[4096,128]{1,0:T(8,128)(2,1)}, u32[]{:S(2)}) copy-start(bf16[4096,128]{1,0:T(8,128)(2,1)} %test_ref.3) | copy-start | bytes 3145732
  85.5 8.6 %collective-permute-start.1 = (f32[16,128,128]{2,1,0:T(8,128)S(1)}, f32[16,128,128]{2,1,0:T(8,128)S(1)}, u32[]{:S(2)}, u32[]{:S(2)}) collective-permute-start(f32[16,128,128]{2,1,0:T(8,128)S(1)} %bitcast.6), channel_id=1, source_target_pairs={{0,4},{4,0},{1,5},{5,1},{2,6},{6,2},{3,7},{7,3},{8,12},{12,8},{9,1... | collective-permute-start | bytes 3145736 | tf_op jit(solution)/shard_map/ppermute | solution.py:314

commit v8 on v7

--- a/solution.py
+++ b/solution.py
@@ -2,6 +2,7 @@
 
 import jax
 import jax.numpy as jnp
+import numpy as np
 from jax import lax
 from jax.experimental import pallas as pl
 from jax.experimental.pallas import tpu as pltpu
@@ -9,6 +10,7 @@
 
 AXES = ("y", "z_pair", "z_in_pair", "core", "x")
 NEAR = ("z_in_pair", "x", "y")
+BACK = ("x", "z_in_pair", "y")
 CHUNKS = 4
 STEP = 2048
 PANEL = 32
@@ -36,16 +38,19 @@
     )
 
 
-def image_blocks(left, right, out, first):
+def image_pieces(left, right, out, first, slots):
     part = dot(left[0], right[0]) + (
         (dot(left[1], right[0]) + dot(left[0], right[1]))
         + (dot(left[2], right[0]) + dot(left[1], right[1]) + dot(left[0], right[2]))
     )
+    height = out.shape[1]
+    cuts = LANES // height
     for b in range(part.shape[1] // LANES):
-        out[first + b] = part[:, b * LANES : (b + 1) * LANES]
-
-
-def sketch_kernel(core_ref, emb_hbm, test_hbm, sketch_ref, send_ref, keep_terms, emb, test, send_terms, sems):
+        for h in range(cuts):
+            out[slots[(first + b) * cuts + h]] = part[h * height : (h + 1) * height, b * LANES : (b + 1) * LANES]
+
+
+def sketch_kernel(slots, core_ref, emb_hbm, test_hbm, sketch_ref, send_ref, keep_terms, emb, test, send_terms, sems):
     rows, width = emb.shape
     columns = width // CHUNKS
     core = core_ref[0]
@@ -75,24 +80,26 @@
     sketch_ref[...] = sketch
     left = split(sketch.T)
     for start in range(0, width // 2, STEP):
-        image_blocks(left, [send_terms[t, :, start : start + STEP] for t in range(3)], send_ref, start // LANES)
-
-
-def keep_kernel(sketch_ref, keep_terms, keep_ref):
+        right = [send_terms[t, :, start : start + STEP] for t in range(3)]
+        image_pieces(left, right, send_ref, start // LANES, slots)
+
+
+def keep_kernel(slots, sketch_ref, keep_terms, keep_ref):
     left = split(sketch_ref[...].T)
     for start in range(0, keep_terms.shape[2], STEP):
-        image_blocks(left, [keep_terms[t, :, start : start + STEP] for t in range(3)], keep_ref, start // LANES)
-
-
-def local_sketch(core, embeddings, test_matrix):
+        right = [keep_terms[t, :, start : start + STEP] for t in range(3)]
+        image_pieces(left, right, keep_ref, start // LANES, slots)
+
+
+def local_sketch(core, embeddings, test_matrix, slots):
     rows, width = embeddings.shape
     half = width // 2
     vmem = pl.BlockSpec(memory_space=pltpu.VMEM)
     return pl.pallas_call(
-        sketch_kernel,
+        functools.partial(sketch_kernel, slots),
         out_shape=[
             pltpu.VMEM((rows, LANES), F32),
-            pltpu.VMEM((half // LANES, LANES, LANES), F32),
+            pltpu.VMEM((len(slots), half // len(slots), LANES), F32),
             pltpu.VMEM((3, rows, half), BF16),
         ],
         in_specs=[
@@ -117,12 +124,12 @@
     )
 
 
-def keep_image(sketch, keep_terms):
+def keep_image(sketch, keep_terms, slots):
     rows, half = keep_terms.shape[1:]
     vmem = pl.BlockSpec(memory_space=pltpu.VMEM)
     return pl.pallas_call(
-        keep_kernel,
-        out_shape=pltpu.VMEM((half // LANES, LANES, LANES), F32),
+        functools.partial(keep_kernel, slots),
+        out_shape=pltpu.VMEM((len(slots), half // len(slots), LANES), F32),
         in_specs=[vmem] * 2,
         out_specs=vmem,
         compiler_params=pltpu.CompilerParams(vmem_limit_bytes=VMEM_LIMIT),
@@ -300,10 +307,11 @@
     return lax.all_to_all(values, axes, 0, 0, tiled=False)
 
 
-def scatter_sum(values, axes):
-    parts = lax.axis_size(axes)
-    blocks = values.reshape((parts, values.shape[0] // parts) + values.shape[1:])
-    return jnp.sum(exchange(blocks, axes), axis=0)
+def slots_of_pieces():
+    sizes = [lax.axis_size(axis) for axis in BACK]
+    order = [BACK.index(axis) for axis in NEAR]
+    places = np.arange(np.prod(sizes)).reshape([sizes[i] for i in order])
+    return [int(place) for place in places.transpose(np.argsort(order)).reshape(-1)]
 
 
 def copies(values, axes):
@@ -319,12 +327,13 @@
     rows, width = embeddings.shape
     own_rows = width // devices_all
     core = lax.axis_index("core")
-    sketch, send, keep_terms = local_sketch(core.reshape(1), embeddings, test_matrix)
+    slots = slots_of_pieces()
+    sketch, send, keep_terms = local_sketch(core.reshape(1), embeddings, test_matrix, slots)
     arriving = swap_cores(send)
-    image = keep_image(sketch, keep_terms) + arriving
-    piece = scatter_sum(image.reshape(-1, LANES), NEAR)
+    image = keep_image(sketch, keep_terms, slots) + arriving
+    piece = jnp.sum(exchange(image, NEAR), axis=0)
     piece = jnp.sum(copies(piece, "z_pair"), axis=0)
-    mine = copies(piece, NEAR).reshape(image.shape)
+    mine = copies(piece, BACK).reshape(-1, LANES, LANES)
     other = swap_cores(mine)
     mine_grams = half_grams(core, mine, test_matrix)
     other_grams = half_grams(1 - core, other, test_matrix)

time: 108 us -> 108 us (level)
  starting transfers between devices: 15.1 us -> 13.8 us
  blocking collectives: 68.9 us -> 70.1 us
    ppermute x2, starting transfers between devices: 15.1 us -> 13.8 us  [swap_cores(): return lax.ppermute(values, 'core', [(0, 1), (1, 0)])]
    all_to_all x3, blocking collectives: 68.9 us -> 70.1 us  [exchange(): return lax.all_to_all(values, axes, 0, 0, tiled=False)]
where the time goes in v8:
time: 108 us
  blocking collectives  70.1 us (65%)
  Pallas kernels  20.8 us (19%)
  starting transfers between devices  13.8 us (13%)
  waiting for transfers between devices  2.15 us (2%)
    all_to_all x3, blocking collectives, exchange(): return lax.all_to_all(values, axes, 0, 0, tiled=False)  70.1 us
    ppermute x2, starting transfers between devices, swap_cores(): return lax.ppermute(values, 'core', [(0, 1), (1, 0)])  13.8 us
    pallas_call x1, Pallas kernels, finish(): pl.pallas_call(functools.partial(finish_kernel, total_rows), out_shape=[j...  12.8 us
    pallas_call x1, Pallas kernels, local_sketch(): pl.pallas_call(functools.partial(sketch_kernel, slots), out_shape=[pltpu....  4.48 us
    pallas_call x2, Pallas kernels, half_grams(): pl.pallas_call(grams_kernel, out_shape=pltpu.VMEM((2, LANES, LANES), F32)...  2.45 us
  transfers between devices with their start and end apart: 2, of which 2 were waited for; matrix products, arithmetic and copies ran while one was open for 0% of the time, Pallas kernels for 2%

profile of v8, /device:TPU:1, one launch (start us, length us, event | category | flops | bytes accessed | tf_op | source)
XLA Modules:
  0.0 108.0 jit_solution(10837686575379027136)
XLA Ops:
  0.6 4.5 %local_sketch.1 = (f32[224,128]{1,0:T(8,128)S(1)}, f32[32,64,128]{2,1,0:T(8,128)S(1)}, bf16[3,224,2048]{2,1,0:T(8,128)(2,1)S(1)}) custom-call(s32[1]{0:T(128)} %bitcast.core_ref.half_ref, f32[224,4096]{1,0:T(8,128)} %emb_hbm.1, bf16[4096,128]{1,0:T(8,128)(2,1)} %test_ref.3), custom_call_target="tpu_custom_call" | custom-call | flops 1409286144 | bytes 3670016 | tf_op jit(solution)/shard_map/local_sketch/pallas_call | solution.py:98
  5.1 8.8 %collective-permute-start = (f32[32,64,128]{2,1,0:T(8,128)S(1)}, f32[32,64,128]{2,1,0:T(8,128)S(1)}, u32[]{:S(2)}, u32[]{:S(2)}) collective-permute-start(f32[32,64,128]{2,1,0:T(8,128)S(1)} %get-tuple-element.8), channel_id=1, source_target_pairs={{0,4},{4,0},{1,5},{5,1},{2,6},{6,2},{3,7},{7,3},{8,12},{12,8},{9,1... | collective-permute-start | bytes 3145736 | tf_op jit(solution)/shard_map/ppermute | solution.py:322
  13.9 1.0 keep_image.1
  15.0 1.2 %collective-permute-done = f32[32,64,128]{2,1,0:T(8,128)S(1)} collective-permute-done((f32[32,64,128]{2,1,0:T(8,128)S(1)}, f32[32,64,128]{2,1,0:T(8,128)S(1)}, u32[]{:S(2)}, u32[]{:S(2)}) %collective-permute-start) | collective-permute-done | bytes 1048608 | tf_op jit(solution)/shard_map/ppermute | solution.py:322
  16.2 0.2 add.25
  16.4 0.0 copy-start
  16.4 18.4 %all_to_all.15 = f32[32,64,128]{2,1,0:T(8,128)S(1)} all-to-all(f32[32,64,128]{2,1,0:T(8,128)S(1)} %add.25), channel_id=1, replica_groups=mesh['y'=4,'z_pair'=8,'z_in_pair'=2,'core'=2,'x'=4] {'z_in_pair','x','y'}, dimensions={0} | all-to-all | bytes 2097152 | tf_op jit(solution)/shard_map/all_to_all | solution.py:307
  34.8 0.1 reduce_sum.18
  34.9 30.2 %all_to_all.16 = f32[8,64,128]{2,1,0:T(8,128)S(1)} all-to-all(f32[8,64,128]{2,1,0:T(8,128)S(1)} %broadcast_in_dim.4), channel_id=1, replica_groups=mesh['y'=4,'z_pair'=8,'z_in_pair'=2,'core'=2,'x'=4] {'z_pair'}, dimensions={0} | all-to-all | bytes 524288 | tf_op jit(solution)/shard_map/all_to_all | solution.py:307
  65.1 0.1 broadcast_in_dim.5
  65.2 21.5 %all_to_all.17 = f32[32,64,128]{2,1,0:T(8,128)S(1)} all-to-all(f32[32,64,128]{2,1,0:T(8,128)S(1)} %broadcast_in_dim.5), channel_id=1, replica_groups=mesh['y'=4,'z_pair'=8,'z_in_pair'=2,'core'=2,'x'=4] {'x','z_in_pair','y'}, dimensions={0} | all-to-all | bytes 2097152 | tf_op jit(solution)/shard_map/all_to_all | solution.py:307
  86.7 5.0 %collective-permute-start.1 = (f32[16,128,128]{2,1,0:T(8,128)S(1)}, f32[16,128,128]{2,1,0:T(8,128)S(1)}, u32[]{:S(2)}, u32[]{:S(2)}) collective-permute-start(f32[16,128,128]{2,1,0:T(8,128)S(1)} %bitcast.5), channel_id=1, source_target_pairs={{0,4},{4,0},{1,5},{5,1},{2,6},{6,2},{3,7},{7,3},{8,12},{12,8},{9,1... | collective-permute-start | bytes 3145736 | tf_op jit(solution)/shard_map/ppermute | solution.py:322
  91.8 0.1 pad_add_fusion.place_ref
  91.8 0.0 copy-done
  91.8 1.2 %half_grams.2.mine_grams = f32[2,128,128]{2,1,0:T(8,128)S(1)} custom-call(s32[1]{0:T(128)} %bitcast.core_ref.half_ref, f32[16,128,128]{2,1,0:T(8,128)S(1)} %bitcast.6, bf16[4096,128]{1,0:T(8,128)(2,1)S(1)} %copy-done), custom_call_target="tpu_custom_call" | custom-call | flops 469762048 | bytes 1048576 | tf_op jit(solution)/shard_map/half_grams/pallas_call | solution.py:226
  93.1 0.9 collective-permute-done.1.ref.other_ref
  94.0 1.2 %half_grams.3.other_grams = f32[2,128,128]{2,1,0:T(8,128)S(1)} custom-call(s32[1]{0:T(128)} %bitcast.4.half_ref, f32[16,128,128]{2,1,0:T(8,128)S(1)} %collective-permute-done.1.ref.other_ref, bf16[4096,128]{1,0:T(8,128)(2,1)S(1)} %copy-done), custom_call_target="tpu_custom_call" | custom-call | flops 469762048 | bytes 1048576 | tf_op jit(solution)/shard_map/half_grams/pallas_call | solution.py:226
  95.2 12.8 %finish.1 = (f32[224,128]{1,0:T(8,128)}, f32[8,128]{1,0:T(8,128)}, f32[128,128]{1,0:T(8,128)}) custom-call(s32[3]{0:T(128)S(1)} %pad_add_fusion.place_ref, f32[2,128,128]{2,1,0:T(8,128)S(1)} %half_grams.2.mine_grams, f32[2,128,128]{2,1,0:T(8,128)S(1)} %half_grams.3.other_grams, f32[16,128,128]{2,1,0:T(8,128)S(1)} %bitcast.7, ...), custom_call_target="tpu_custom_call" | custom-call | tf_op jit(solution)/shard_map/finish/pallas_call | solution.py:287
  (2 shorter events, 0.0 us)
Async XLA Ops:
  5.1 11.1 %collective-permute-start = (f32[32,64,128]{2,1,0:T(8,128)S(1)}, f32[32,64,128]{2,1,0:T(8,128)S(1)}, u32[]{:S(2)}, u32[]{:S(2)}) collective-permute-start(f32[32,64,128]{2,1,0:T(8,128)S(1)} %get-tuple-element.8), channel_id=1, source_target_pairs={{0,4},{4,0},{1,5},{5,1},{2,6},{6,2},{3,7},{7,3},{8,12},{12,8},{9,1... | collective-permute-start | bytes 3145736 | tf_op jit(solution)/shard_map/ppermute | solution.py:322
  16.4 75.5 %copy-start = (bf16[4096,128]{1,0:T(8,128)(2,1)S(1)}, bf16[4096,128]{1,0:T(8,128)(2,1)}, u32[]{:S(2)}) copy-start(bf16[4096,128]{1,0:T(8,128)(2,1)} %test_ref.3) | copy-start | bytes 3145732
  86.7 7.3 %collective-permute-start.1 = (f32[16,128,128]{2,1,0:T(8,128)S(1)}, f32[16,128,128]{2,1,0:T(8,128)S(1)}, u32[]{:S(2)}, u32[]{:S(2)}) collective-permute-start(f32[16,128,128]{2,1,0:T(8,128)S(1)} %bitcast.5), channel_id=1, source_target_pairs={{0,4},{4,0},{1,5},{5,1},{2,6},{6,2},{3,7},{7,3},{8,12},{12,8},{9,1... | collective-permute-start | bytes 3145736 | tf_op jit(solution)/shard_map/ppermute | solution.py:322

commit v9 on v8

--- a/solution.py
+++ b/solution.py
@@ -8,7 +8,8 @@
 from jax.experimental.pallas import tpu as pltpu
 from jax.sharding import Mesh, PartitionSpec as P
 
-AXES = ("y", "z_pair", "z_in_pair", "core", "x")
+AXES = ("y", "z_half", "z_pair", "z_in_pair", "core", "x")
+FAR = ("z_pair", "z_half")
 NEAR = ("z_in_pair", "x", "y")
 BACK = ("x", "z_in_pair", "y")
 CHUNKS = 4
@@ -332,7 +333,7 @@
     arriving = swap_cores(send)
     image = keep_image(sketch, keep_terms, slots) + arriving
     piece = jnp.sum(exchange(image, NEAR), axis=0)
-    piece = jnp.sum(copies(piece, "z_pair"), axis=0)
+    piece = jnp.sum(copies(piece, FAR), axis=0)
     mine = copies(piece, BACK).reshape(-1, LANES, LANES)
     other = swap_cores(mine)
     mine_grams = half_grams(core, mine, test_matrix)
@@ -344,7 +345,7 @@
 
 
 def solution(mesh):
-    fine = Mesh(mesh.devices.reshape(4, 8, 2, 2, 4), AXES)
+    fine = Mesh(mesh.devices.reshape(4, 2, 4, 2, 2, 4), AXES)
     return jax.shard_map(
         per_device,
         mesh=fine,

time: 108 us -> 107 us (level)
  no operation moved by 1% of the time
where the time goes in v9:
time: 107 us
  blocking collectives  69.7 us (65%)
  Pallas kernels  20.8 us (19%)
  starting transfers between devices  13 us (12%)
  waiting for transfers between devices  2.15 us (2%)
    all_to_all x3, blocking collectives, exchange(): return lax.all_to_all(values, axes, 0, 0, tiled=False)  69.7 us
    ppermute x2, starting transfers between devices, swap_cores(): return lax.ppermute(values, 'core', [(0, 1), (1, 0)])  13 us
    pallas_call x1, Pallas kernels, finish(): pl.pallas_call(functools.partial(finish_kernel, total_rows), out_shape=[j...  12.8 us
    pallas_call x1, Pallas kernels, local_sketch(): pl.pallas_call(functools.partial(sketch_kernel, slots), out_shape=[pltpu....  4.48 us
    pallas_call x2, Pallas kernels, half_grams(): pl.pallas_call(grams_kernel, out_shape=pltpu.VMEM((2, LANES, LANES), F32)...  2.45 us
    ppermute x2, waiting for transfers between devices, swap_cores(): return lax.ppermute(values, 'core', [(0, 1), (1, 0)])  2.15 us
  transfers between devices with their start and end apart: 2, of which 2 were waited for; matrix products, arithmetic and copies ran while one was open for 0% of the time, Pallas kernels for 2%

profile of v9, /device:TPU:1, one launch (start us, length us, event | category | flops | bytes accessed | tf_op | source)
XLA Modules:
  0.0 106.8 jit_solution(14162827994447953046)
XLA Ops:
  0.6 4.5 %local_sketch.1 = (f32[224,128]{1,0:T(8,128)S(1)}, f32[32,64,128]{2,1,0:T(8,128)S(1)}, bf16[3,224,2048]{2,1,0:T(8,128)(2,1)S(1)}) custom-call(s32[1]{0:T(128)} %bitcast.core_ref.half_ref, f32[224,4096]{1,0:T(8,128)} %emb_hbm.1, bf16[4096,128]{1,0:T(8,128)(2,1)} %test_ref.3), custom_call_target="tpu_custom_call" | custom-call | flops 1409286144 | bytes 3670016 | tf_op jit(solution)/shard_map/local_sketch/pallas_call | solution.py:99
  5.1 8.8 %collective-permute-start = (f32[32,64,128]{2,1,0:T(8,128)S(1)}, f32[32,64,128]{2,1,0:T(8,128)S(1)}, u32[]{:S(2)}, u32[]{:S(2)}) collective-permute-start(f32[32,64,128]{2,1,0:T(8,128)S(1)} %get-tuple-element.8), channel_id=1, source_target_pairs={{0,4},{4,0},{1,5},{5,1},{2,6},{6,2},{3,7},{7,3},{8,12},{12,8},{9,1... | collective-permute-start | bytes 3145736 | tf_op jit(solution)/shard_map/ppermute | solution.py:323
  13.9 1.0 keep_image.1
  15.0 1.2 %collective-permute-done = f32[32,64,128]{2,1,0:T(8,128)S(1)} collective-permute-done((f32[32,64,128]{2,1,0:T(8,128)S(1)}, f32[32,64,128]{2,1,0:T(8,128)S(1)}, u32[]{:S(2)}, u32[]{:S(2)}) %collective-permute-start) | collective-permute-done | bytes 1048608 | tf_op jit(solution)/shard_map/ppermute | solution.py:323
  16.2 0.2 add.29
  16.4 0.0 copy-start
  16.4 18.4 %all_to_all.15 = f32[32,64,128]{2,1,0:T(8,128)S(1)} all-to-all(f32[32,64,128]{2,1,0:T(8,128)S(1)} %add.29), channel_id=1, replica_groups=mesh['y'=4,'z_half'=2,'z_pair'=4,'z_in_pair'=2,'core'=2,'x'=4] {'z_in_pa..., dimensions={0} | all-to-all | bytes 2097152 | tf_op jit(solution)/shard_map/all_to_all | solution.py:308
  34.8 0.1 reduce_sum.18
  34.9 25.7 %all_to_all.16 = f32[8,64,128]{2,1,0:T(8,128)S(1)} all-to-all(f32[8,64,128]{2,1,0:T(8,128)S(1)} %broadcast_in_dim.4), channel_id=1, replica_groups=mesh['y'=4,'z_half'=2,'z_pair'=4,'z_in_pair'=2,'core'=2,'x'=4] {'z_pair'..., dimensions={0} | all-to-all | bytes 524288 | tf_op jit(solution)/shard_map/all_to_all | solution.py:308
  60.6 0.1 broadcast_in_dim.5
  60.7 25.6 %all_to_all.17 = f32[32,64,128]{2,1,0:T(8,128)S(1)} all-to-all(f32[32,64,128]{2,1,0:T(8,128)S(1)} %broadcast_in_dim.5), channel_id=1, replica_groups=mesh['y'=4,'z_half'=2,'z_pair'=4,'z_in_pair'=2,'core'=2,'x'=4] {'x','z_i..., dimensions={0} | all-to-all | bytes 2097152 | tf_op jit(solution)/shard_map/all_to_all | solution.py:308
  86.3 4.2 %collective-permute-start.1 = (f32[16,128,128]{2,1,0:T(8,128)S(1)}, f32[16,128,128]{2,1,0:T(8,128)S(1)}, u32[]{:S(2)}, u32[]{:S(2)}) collective-permute-start(f32[16,128,128]{2,1,0:T(8,128)S(1)} %bitcast.5), channel_id=1, source_target_pairs={{0,4},{4,0},{1,5},{5,1},{2,6},{6,2},{3,7},{7,3},{8,12},{12,8},{9,1... | collective-permute-start | bytes 3145736 | tf_op jit(solution)/shard_map/ppermute | solution.py:323
  90.6 0.1 pad_add_fusion.place_ref
  90.7 0.0 copy-done
  90.7 1.2 %half_grams.2.mine_grams = f32[2,128,128]{2,1,0:T(8,128)S(1)} custom-call(s32[1]{0:T(128)} %bitcast.core_ref.half_ref, f32[16,128,128]{2,1,0:T(8,128)S(1)} %bitcast.6, bf16[4096,128]{1,0:T(8,128)(2,1)S(1)} %copy-done), custom_call_target="tpu_custom_call" | custom-call | flops 469762048 | bytes 1048576 | tf_op jit(solution)/shard_map/half_grams/pallas_call | solution.py:227
  91.9 0.9 collective-permute-done.1.ref.other_ref
  92.8 1.2 %half_grams.3.other_grams = f32[2,128,128]{2,1,0:T(8,128)S(1)} custom-call(s32[1]{0:T(128)} %bitcast.4.half_ref, f32[16,128,128]{2,1,0:T(8,128)S(1)} %collective-permute-done.1.ref.other_ref, bf16[4096,128]{1,0:T(8,128)(2,1)S(1)} %copy-done), custom_call_target="tpu_custom_call" | custom-call | flops 469762048 | bytes 1048576 | tf_op jit(solution)/shard_map/half_grams/pallas_call | solution.py:227
  94.0 12.8 %finish.1 = (f32[224,128]{1,0:T(8,128)}, f32[8,128]{1,0:T(8,128)}, f32[128,128]{1,0:T(8,128)}) custom-call(s32[3]{0:T(128)S(1)} %pad_add_fusion.place_ref, f32[2,128,128]{2,1,0:T(8,128)S(1)} %half_grams.2.mine_grams, f32[2,128,128]{2,1,0:T(8,128)S(1)} %half_grams.3.other_grams, f32[16,128,128]{2,1,0:T(8,128)S(1)} %bitcast.7, ...), custom_call_target="tpu_custom_call" | custom-call | tf_op jit(solution)/shard_map/finish/pallas_call | solution.py:288
  (2 shorter events, 0.0 us)
Async XLA Ops:
  5.1 11.1 %collective-permute-start = (f32[32,64,128]{2,1,0:T(8,128)S(1)}, f32[32,64,128]{2,1,0:T(8,128)S(1)}, u32[]{:S(2)}, u32[]{:S(2)}) collective-permute-start(f32[32,64,128]{2,1,0:T(8,128)S(1)} %get-tuple-element.8), channel_id=1, source_target_pairs={{0,4},{4,0},{1,5},{5,1},{2,6},{6,2},{3,7},{7,3},{8,12},{12,8},{9,1... | collective-permute-start | bytes 3145736 | tf_op jit(solution)/shard_map/ppermute | solution.py:323
  16.4 74.3 %copy-start = (bf16[4096,128]{1,0:T(8,128)(2,1)S(1)}, bf16[4096,128]{1,0:T(8,128)(2,1)}, u32[]{:S(2)}) copy-start(bf16[4096,128]{1,0:T(8,128)(2,1)} %test_ref.3) | copy-start | bytes 3145732
  86.3 6.5 %collective-permute-start.1 = (f32[16,128,128]{2,1,0:T(8,128)S(1)}, f32[16,128,128]{2,1,0:T(8,128)S(1)}, u32[]{:S(2)}, u32[]{:S(2)}) collective-permute-start(f32[16,128,128]{2,1,0:T(8,128)S(1)} %bitcast.5), channel_id=1, source_target_pairs={{0,4},{4,0},{1,5},{5,1},{2,6},{6,2},{3,7},{7,3},{8,12},{12,8},{9,1... | collective-permute-start | bytes 3145736 | tf_op jit(solution)/shard_map/ppermute | solution.py:323
